TPU v7x, 32 devices: a whole 2x2x4 slice. The times are simulated.
32 devices in a mesh: seq: 16 (over z, y, x), mp: 2 (over core).
Axes of the slice: x: 2, y: 2, z: 4, core: 2. Of those that a mesh axis runs over, the one named last changes fastest.
Arguments:
- residual_in: bfloat16 [16384, 1024], P('seq'), may hold values from -6 to 6
- query_rows: bfloat16 [16384, 1024], P('seq', 'mp'), may hold values from -6 to 6
- key_rows: bfloat16 [16384, 1024], P('seq', 'mp'), may hold values from -6 to 6
- value_rows: bfloat16 [16384, 1024], P('seq', 'mp'), may hold values from -6 to 6
- rand_blocks: int32 [256, 16, 3], P(None, 'mp'), may hold values from 0 to 255, as said below
- global_blocks: int32 [2], replicated, may hold values from 0 to 255, as said below
- out_weight: bfloat16 [1024, 1024], P('mp'), may hold values from -0.1875 to 0.1875
- norm_gain: float32 [1024], replicated, may hold values from 0.25 to 1.75
- up_weight: bfloat16 [1024, 4096], P(None, 'mp'), may hold values from -0.1875 to 0.1875
- down_weight: bfloat16 [4096, 1024], P('mp'), may hold values from -0.09375 to 0.09375
Outputs:
- layer_out: bfloat16 [16384, 1024], P('seq', 'mp')
Inputs may be any that keep to these rules, and one draw needn't show every extreme that they name: `rand_blocks`: each entry names a block of the same run of 16 consecutive groups of 16 blocks as its query block (groups counted from block 0). For every group of 16 query blocks, every set of 8 consecutive heads starting at a multiple of 8, and every group of its run, exactly 24 entries point into that group. `global_blocks`: the 2 entries differ; the last one is block 255.
All inputs are finite; a program needn't handle non-finite values.
Results may differ from a plain program's by a relative error of at most 0.006.
Values may be sent and summed in bfloat16 or wider, within the bound.
A program may use at most 256 MiB of HBM per device.

v0:
```python
import math

import jax
import jax.numpy as jnp
from jax import lax
from jax.sharding import PartitionSpec as P

HD = 64
BLK = 64
R = 3
GLOB = 2
GROUP = 16
QB_DEV = 16


def with_halo(block, sides, width):
    for axis, dim in sides:
        count = lax.axis_size(axis)
        forward = [(i, i + 1) for i in range(count - 1)]
        backward = [(target, source) for source, target in forward]
        low = lax.ppermute(
            lax.slice_in_dim(block, block.shape[dim] - width, None, axis=dim), axis, forward
        )
        high = lax.ppermute(lax.slice_in_dim(block, 0, width, axis=dim), axis, backward)
        block = jnp.concatenate([low, block, high], axis=dim)
    return block


def swapped(block, axis, apart):
    count = lax.axis_size(axis)
    route = []
    for low in range(count):
        high = low | 1 << apart
        if high != low and high < count:
            route += [(low, high), (high, low)]
    return lax.ppermute(block, axis, route)


def joined(shard, axis, combine):
    everything = jax.tree.map(lambda part: lax.all_gather(part, axis), shard)
    initial = jax.tree.map(lambda part: part[0], everything)

    def hop(k, so_far):
        return combine(so_far, jax.tree.map(lambda part: part[k], everything))

    return lax.fori_loop(1, lax.axis_size(axis), hop, initial)


def combine_parts(first_part, second_part):
    peak_a, total_a, accum_a = first_part
    peak_b, total_b, accum_b = second_part
    larger = jnp.maximum(peak_a, peak_b)
    factor_a = jnp.exp(peak_a - larger)
    factor_b = jnp.exp(peak_b - larger)
    return (
        larger,
        total_a * factor_a + total_b * factor_b,
        accum_a * factor_a[..., None] + accum_b * factor_b[..., None],
    )


def local(
    residual_in,
    query_rows,
    key_rows,
    value_rows,
    rand_blocks,
    global_blocks,
    out_weight,
    norm_gain,
    up_weight,
    down_weight,
):
    tok_rows = query_rows.shape[0]
    local_width = query_rows.shape[1]
    heads_here = local_width // HD
    shard_count = lax.axis_size("seq")
    my_shard = lax.axis_index("seq")
    total_blocks = QB_DEV * shard_count
    score_scale = 1.0 / math.sqrt(HD)
    q_heads = query_rows.reshape(QB_DEV, BLK, heads_here, HD)
    key_heads = key_rows.reshape(tok_rows, heads_here, HD)
    value_heads = value_rows.reshape(tok_rows, heads_here, HD)
    kv_tokens = jnp.concatenate([key_heads, value_heads], axis=2)
    padded = with_halo(kv_tokens, (("seq", 0),), BLK)
    padded_blocks = padded.reshape(QB_DEV + 2, BLK, heads_here, 2 * HD).transpose(0, 2, 1, 3)
    own_blocks = padded_blocks[1:-1]
    window_kv = jnp.stack([padded_blocks[:-2], own_blocks, padded_blocks[2:]], axis=2)
    flat_kv = own_blocks.reshape(QB_DEV * heads_here, BLK, 2 * HD)
    position = my_shard % GROUP
    group_base = my_shard - position
    slot_count = QB_DEV * heads_here * R
    capacity = slot_count // GROUP
    offsets_all = jnp.arange(GROUP, dtype=jnp.int32)
    slot_heads = jnp.arange(slot_count, dtype=jnp.int32) // R % heads_here
    cap_range = jnp.arange(capacity, dtype=jnp.int32)

    def requests_of(shard):
        request_rows = lax.dynamic_slice_in_dim(rand_blocks, shard * QB_DEV, QB_DEV, 0)
        return request_rows.reshape(slot_count)

    def payload_for(offset):
        requester = group_base + (position - offset) % GROUP
        wanted = requests_of(requester)
        from_me = wanted // QB_DEV == my_shard
        order_rank = jnp.cumsum(from_me.astype(jnp.int32)) - 1
        source = wanted % QB_DEV * heads_here + slot_heads
        pick_table = from_me[:, None] & (order_rank[:, None] == cap_range[None, :])
        chosen = jnp.sum(jnp.where(pick_table, source[:, None], 0), axis=0)
        return jnp.take(flat_kv, chosen, axis=0)

    my_requests = requests_of(my_shard)
    owner_offset = (my_requests // QB_DEV - group_base - position) % GROUP
    offset_hits = owner_offset[:, None] == offsets_all[None, :]
    rank_table = jnp.cumsum(offset_hits.astype(jnp.int32), axis=0) - 1
    my_rank = jnp.sum(jnp.where(offset_hits, rank_table, 0), axis=1)
    slot_index = owner_offset * capacity + my_rank
    sectioned = jax.vmap(payload_for)(offsets_all)
    buffer_rows = jnp.take(sectioned, (position - (position ^ offsets_all)) % GROUP, axis=0)
    for bit in range(GROUP.bit_length() - 1):
        moving = jnp.array([slot for slot in range(GROUP) if slot >> bit & 1], dtype=jnp.int32)
        outbound = jnp.take(buffer_rows, moving, axis=0)
        inbound = swapped(outbound, "seq", bit)
        buffer_rows = buffer_rows.at[moving].set(inbound)
    received = jnp.take(buffer_rows, (position + offsets_all) % GROUP ^ position, axis=0)
    random_kv = jnp.take(received.reshape(GROUP * capacity, BLK, 2 * HD), slot_index, axis=0)
    random_kv = random_kv.reshape(QB_DEV, heads_here, R, BLK, 2 * HD)
    packed = jnp.stack([query_rows, key_rows, value_rows], axis=0)
    contributions = []
    for which in range(GLOB):
        global_id = global_blocks[which]
        block_rows = lax.dynamic_slice_in_dim(packed, global_id % QB_DEV * BLK, BLK, 1).astype(
            jnp.float32
        )
        is_owner = global_id // QB_DEV == my_shard
        contributions.append(jnp.where(is_owner, block_rows, 0.0))
    summed_rows = lax.psum(jnp.stack(contributions, axis=0), "seq")
    global_packed = summed_rows.astype(jnp.bfloat16)
    global_q = global_packed[:, 0].reshape(GLOB, BLK, heads_here, HD)
    global_k = global_packed[:, 1].reshape(GLOB, BLK, heads_here, HD)
    global_v = global_packed[:, 2].reshape(GLOB, BLK, heads_here, HD)
    global_kv = jnp.concatenate([global_k, global_v], axis=3).transpose(2, 0, 1, 3)
    global_kv = jnp.broadcast_to(global_kv[None], (QB_DEV, heads_here, GLOB, BLK, 2 * HD))
    all_kv = jnp.concatenate([window_kv, random_kv, global_kv], axis=2)
    keys_all = all_kv[..., :HD]
    values_all = all_kv[..., HD:]
    scores = (
        jnp.einsum("bqhd,bhjkd->bhqjk", q_heads, keys_all, preferred_element_type=jnp.float32)
        * score_scale
    )
    block_global = my_shard * QB_DEV + jnp.arange(QB_DEV, dtype=jnp.int32)
    valid_cols = jnp.concatenate(
        [
            (block_global >= 1)[:, None],
            jnp.ones((QB_DEV, 1), dtype=bool),
            (block_global + 1 < total_blocks)[:, None],
            jnp.ones((QB_DEV, R + GLOB), dtype=bool),
        ],
        axis=1,
    )
    scores = jnp.where(valid_cols[:, None, None, :, None], scores, jnp.float32(-1e30))
    row_peak = jnp.max(scores, axis=(3, 4), keepdims=True)
    weights = jnp.exp(scores - row_peak)
    row_total = jnp.sum(weights, axis=(3, 4))
    mixed_sum = jnp.einsum(
        "bhqjk,bhjkd->bqhd",
        weights.astype(jnp.bfloat16),
        values_all,
        preferred_element_type=jnp.float32,
    )
    sparse_out = mixed_sum / row_total.transpose(0, 2, 1)[..., None]
    global_scores = (
        jnp.einsum("gqhd,thd->ghqt", global_q, key_heads, preferred_element_type=jnp.float32)
        * score_scale
    )
    seg_peak = jnp.max(global_scores, axis=3)
    seg_weights = jnp.exp(global_scores - seg_peak[..., None])
    seg_total = jnp.sum(seg_weights, axis=3)
    seg_acc = jnp.einsum(
        "ghqt,thd->ghqd",
        seg_weights.astype(jnp.bfloat16),
        value_heads,
        preferred_element_type=jnp.float32,
    )
    merged_peak, merged_total, merged_acc = joined(
        (seg_peak, seg_total, seg_acc), "seq", combine_parts
    )
    global_out = merged_acc / merged_total[..., None]
    attn_rows = sparse_out.reshape(tok_rows, local_width)
    for which in range(GLOB):
        global_id = global_blocks[which]
        start_row = global_id % QB_DEV * BLK
        current = lax.dynamic_slice_in_dim(attn_rows, start_row, BLK, 0)
        replacing = global_out[which].transpose(1, 0, 2).reshape(BLK, local_width)
        is_owner = global_id // QB_DEV == my_shard
        attn_rows = lax.dynamic_update_slice_in_dim(
            attn_rows, jnp.where(is_owner, replacing, current), start_row, 0
        )
    attention = attn_rows.astype(jnp.bfloat16)
    projected = jnp.dot(attention, out_weight, preferred_element_type=jnp.float32)
    mp_index = lax.axis_index("mp")
    half_width = residual_in.shape[1] // lax.axis_size("mp")
    attn_full = lax.psum(projected, "mp")
    middle = (residual_in.astype(jnp.float32) + attn_full).astype(jnp.bfloat16)
    middle_own = lax.dynamic_slice_in_dim(middle, mp_index * half_width, half_width, 1)
    middle32 = middle.astype(jnp.float32)
    row_mean = jnp.mean(middle32, axis=1, keepdims=True)
    centered = middle32 - row_mean
    row_var = jnp.mean(centered * centered, axis=1, keepdims=True)
    normed = (centered * lax.rsqrt(row_var + 1e-05) * norm_gain).astype(jnp.bfloat16)
    hidden = jax.nn.gelu(
        jnp.dot(normed, up_weight, preferred_element_type=jnp.float32), approximate=True
    ).astype(jnp.bfloat16)
    down_out = jnp.dot(hidden, down_weight, preferred_element_type=jnp.float32)
    down_part = lax.psum_scatter(down_out, "mp", scatter_dimension=1, tiled=True)
    return (middle_own.astype(jnp.float32) + down_part).astype(jnp.bfloat16)


def solution(mesh):
    placed = (
        P("seq", None),
        P("seq", "mp"),
        P("seq", "mp"),
        P("seq", "mp"),
        P(None, "mp", None),
        P(),
        P("mp", None),
        P(),
        P(None, "mp"),
        P("mp", None),
    )
    return jax.shard_map(
        local, mesh=mesh, in_specs=placed, out_specs=P("seq", "mp"), check_vma=False
    )
```

profile of v0, /device:TPU:17, one launch (start us, length us, event | category | flops | bytes accessed | tf_op | source)
XLA Modules:
  0.0 799.2 jit_solution(16351259633467382436)
XLA Ops:
  11.1 4.0 collective-permute-start.1
  23.4 2.7 gather_fusion
  34.9 2.2 pad_maximum_fusion
  38.2 4.7 concatenate.20
  43.0 2.8 copy.131
  45.8 2.3 copy.195
  49.7 5.6 gather_fusion.1
  55.3 6.7 broadcast_select_fusion.2
  62.0 6.8 gather_fusion.3
  68.8 6.2 broadcast_select_fusion.1
  75.0 5.4 gather_fusion.4
  81.9 124.1 %all-reduce.5 = bf16[2,3,64,512]{3,2,1,0:T(8,128)(2,1)} all-reduce(f32[2,3,64,512]{3,2,1,0:T(8,128)} %pad_maximum_fusion.2), channel_id=1, replica_groups=mesh['seq'=16,'mp'=2] {'seq'}, use_global_device_ids=true, to_apply=%region_10.13 | all-reduce | flops 196608 | bytes 1179648 | tf_op jit(solution)/shard_map/psum | solution.py:137
  209.5 2.2 bitcast_reduce_fusion.1
  215.7 9.8 %scatter_fusion = bf16[16,24,64,128]{3,2,1,0:T(8,128)(2,1)} fusion(bf16[16,24,64,128]{3,2,1,0:T(8,128)(2,1)} %broadcast_select_fusion.1, s32[8]{0:T(128)S(1)} %copy-done.20, bf16[8,24,64,128]{3,2,1,0:T(8,128)(2,1)} %collective-permute-done.2), kind=kCustom, calls=%fused_computation.9 | custom fusion | bytes 9437216 | tf_op jit(solution)/shard_map/scatter | solution.py:124
  225.5 5.4 gather_fusion.5
  233.2 3.9 reshape.459
  239.6 59.0 %collective-permute-done.3 = bf16[8,24,64,128]{3,2,1,0:T(8,128)(2,1)} collective-permute-done((bf16[8,24,64,128]{3,2,1,0:T(8,128)(2,1)}, bf16[8,24,64,128]{3,2,1,0:T(8,128)(2,1)}, u32[]{:S(2)}, u32[]{:S(2)}) %collective-permute-start.3) | collective-permute-done | bytes 3145760 | tf_op jit(solution)/shard_map/ppermute | solution.py:36
  298.5 10.3 %scatter_fusion.1 = bf16[16,24,64,128]{3,2,1,0:T(8,128)(2,1)} fusion(bf16[16,24,64,128]{3,2,1,0:T(8,128)(2,1)} %scatter_fusion, s32[8]{0:T(128)S(1)} %copy-done.19, bf16[8,24,64,128]{3,2,1,0:T(8,128)(2,1)} %collective-permute-done.3), kind=kCustom, calls=%fused_computation.10 | custom fusion | bytes 9437216 | tf_op jit(solution)/shard_map/scatter | solution.py:124
  308.8 5.5 gather_fusion.6
  314.4 7.7 collective-permute-start.4
  325.9 2.6 reduce-window.14
  340.3 3.1 fusion.33
  343.4 77.0 %all-gather.1 = f32[32,8,64]{2,1,0:T(8,128)S(1)} all-gather(f32[2,8,64]{2,1,0:T(8,128)S(1)} %copy.163), channel_id=3, replica_groups=mesh['seq'=16,'mp'=2] {'seq'}, dimensions={0}, use_global_device_ids=true | all-gather | bytes 69632 | tf_op jit(solution)/shard_map/all_gather | solution.py:40
  420.4 25.7 %all-gather = f32[32,8,64]{2,1,0:T(8,128)S(1)} all-gather(f32[2,8,64]{2,1,0:T(8,128)} %copy.162), channel_id=2, replica_groups=mesh['seq'=16,'mp'=2] {'seq'}, dimensions={0}, use_global_device_ids=true | all-gather | bytes 69632 | tf_op jit(solution)/shard_map/all_gather | solution.py:40
  452.6 2.0 fusion.43
  454.7 2.0 bitcast_dynamic-update-slice_fusion
  459.8 10.2 %scatter_fusion.2 = bf16[16,24,64,128]{3,2,1,0:T(8,128)(2,1)} fusion(bf16[16,24,64,128]{3,2,1,0:T(8,128)(2,1)} %scatter_fusion.1, s32[8]{0:T(128)} %constant.281.clone, bf16[8,24,64,128]{3,2,1,0:T(8,128)(2,1)} %collective-permute-done.4), kind=kCustom, calls=%fused_computation.11 | custom fusion | bytes 9437216 | tf_op jit(solution)/shard_map/scatter | solution.py:124
  470.0 5.5 gather_fusion.7
  475.5 11.9 %collective-permute-start.5 = (bf16[8,24,64,128]{3,2,1,0:T(8,128)(2,1)}, bf16[8,24,64,128]{3,2,1,0:T(8,128)(2,1)}, u32[]{:S(2)}, u32[]{:S(2)}) collective-permute-start(bf16[8,24,64,128]{3,2,1,0:T(8,128)(2,1)} %gather_fusion.7), channel_id=1, source_target_pairs={{0,16},{16,0},{2,18},{18,2},{4,20},{20,4},{6,22},{22,6},{8,24},{24... | collective-permute-start | bytes 9437192 | tf_op jit(solution)/shard_map/ppermute | solution.py:36
  487.4 34.4 %while.19 = (s32[]{:T(128)}, f32[2,8,64]{2,1,0:T(8,128)S(1)}, f32[2,8,64]{2,1,0:T(8,128)S(1)}, f32[2,8,64,64]{3,2,1,0:T(8,128)S(1)}, f32[16,2,8,64]{3,2,1,0:T(8,...) while((s32[]{:T(128)}, f32[2,8,64]{2,1,0:T(8,128)S(1)}, ...), condition=%wide.region_16.19_spmd, body=%wide.region_15.18_spmd.sunk | while | flops 202757 | bytes 1089679 | solution.py:46
  522.5 95.0 %collective-permute-done.5 = bf16[8,24,64,128]{3,2,1,0:T(8,128)(2,1)} collective-permute-done((bf16[8,24,64,128]{3,2,1,0:T(8,128)(2,1)}, bf16[8,24,64,128]{3,2,1,0:T(8,128)(2,1)}, u32[]{:S(2)}, u32[]{:S(2)}) %collective-permute-start.5) | collective-permute-done | bytes 3145760 | tf_op jit(solution)/shard_map/ppermute | solution.py:36
  617.6 9.8 %scatter_fusion.3 = bf16[16,24,64,128]{3,2,1,0:T(8,128)(2,1)} fusion(bf16[16,24,64,128]{3,2,1,0:T(8,128)(2,1)} %scatter_fusion.2, s32[8]{0:T(128)S(1)} %copy-done.17, bf16[8,24,64,128]{3,2,1,0:T(8,128)(2,1)} %collective-permute-done.5), kind=kCustom, calls=%fused_computation.12 | custom fusion | bytes 9437216 | tf_op jit(solution)/shard_map/scatter | solution.py:124
  627.4 6.8 gather_fusion.8
  634.2 6.0 broadcast_select_fusion
  640.2 6.8 gather_fusion.2
  647.1 7.1 select_dynamic-update-slice_fusion
  654.2 3.0 broadcast_dynamic-update-slice_fusion
  657.2 18.2 %bitcast_reduce_fusion = (f32[16,8,64]{2,1,0:T(8,128)S(1)}, f32[16,8,8,64,64]{4,3,2,1,0:T(8,128)}) fusion(pred[16,8]{1,0:T(8,128)(4,1)S(1)} %copy-done.14, bf16[16,64,8,64,1]{3,2,1,0,4:T(8,128)(2,1)S(1)} %bitcast.177, bf16[16,8,8,64,128]{4,3,2,1,0:T(8,128)(2,1)} %broadcast_dynamic-update-slice_fusion), kind=kOutput, calls=%fused_computation.24 | convolution fusion | flops 549445632 | bytes 34635904 | tf_op jit(solution)/shard_map/bqhd,bhjkd->bhqjk/dot_general | solution.py:148
  675.4 14.9 %fusion.5 = f32[16,8,64]{2,1,0:T(8,128)S(1)} fusion(f32[16,8,8,64,64]{4,3,2,1,0:T(8,128)} %get-tuple-element.253, f32[16,8,64]{2,1,0:T(8,128)S(1)} %get-tuple-element.252, pred[16,8]{1,0:T(8,128)(4,1)S(1)} %copy-done.14), kind=kLoop, calls=%fused_computation.27 | loop fusion | flops 16769024 | bytes 16842880 | tf_op jit(solution)/shard_map/reduce_sum | solution.py:164
  690.3 21.7 %bitcast_divide_fusion = bf16[16,64,8,64]{1,3,2,0:T(8,128)(2,1)} fusion(f32[16,8,8,64,64]{4,3,2,1,0:T(8,128)} %get-tuple-element.253, f32[16,8,64]{2,1,0:T(8,128)S(1)} %get-tuple-element.252, pred[16,8]{1,0:T(8,128)(4,1)S(1)} %copy-done.14, bf16[16,8,8,64,128]{4,3,2,1,0:T(8,128)(2,1)} %broadcast_dynamic-update-slice_fusion, f32[16,64,8]{1,2,0:T(8,128)S(1)} %bitcast.181), kind=kOutput, calls=%fused_computation.57 | convolution fusion | flops 554696704 | bytes 34668672 | tf_op jit(solution)/shard_map/bhqjk,bhjkd->bqhd/dot_general | solution.py:165
  712.0 3.5 copy.160
  715.5 2.0 reshape.460
  720.5 4.4 fusion.121
  725.0 32.2 %all-reduce.4.cloned.1.call-done = f32[1024,1024]{1,0:T(8,128)} async-done(((f32[1024,1024]{1,0:T(8,128)}), f32[1024,1024]{1,0:T(8,128)}) %all-reduce.4.cloned.1.call-update) | async-done | bytes 4194320 | tf_op jit(solution)/shard_map/psum | solution.py:203
  757.2 3.4 convert_reduce_fusion
  761.4 14.5 %fusion.30 = f32[1024,1024]{1,0:T(8,128)} fusion(bf16[2048,1024]{1,0:T(8,128)(2,1)} %param.29, bf16[1024,2048]{1,0:T(8,128)(2,1)} %param.28, bf16[1024,1024]{1,0:T(8,128)(2,1)S(1)} %get-tuple-element.240, f32[1024]{0:T(1024)S(1)} %copy-done.23, f32[1024]{0:T(1024)S(1)} %add_rsqrt_fusion, f32[1024]{0:T(1024)S(1)} %broadcast_multiply_fusion), kind=kOutput, calls=%fused_computation.62 | convolution fusion | flops 8614051840 | bytes 14692352 | tf_op jit(solution)/shard_map/dot_general | solution.py:214
  775.9 13.4 %reduce-scatter.2.cloned.1.call-done = f32[1024,512]{1,0:T(8,128)} async-done(((f32[1024,1024]{1,0:T(8,128)}), f32[1024,512]{1,0:T(8,128)}) %reduce-scatter.2.cloned.1.call-update) | async-done | bytes 2097168 | tf_op jit(solution)/shard_map/reduce_scatter | solution.py:215
  789.2 3.0 add_convert_fusion.1
  (178 shorter events, 97.1 us)
Async XLA Ops:
  6.5 714.0 %copy-start = (bf16[512,1024]{1,0:T(8,128)(2,1)S(1)}, bf16[512,1024]{1,0:T(8,128)(2,1)}, u32[]{:S(2)}) copy-start(bf16[512,1024]{1,0:T(8,128)(2,1)} %param.26) | copy-start | bytes 3145732
  6.5 10.5 %copy-start.21 = (s32[2]{0:T(128)S(1)}, s32[2]{0:T(128)}, u32[]{:S(2)}) copy-start(s32[2]{0:T(128)} %param.25) | copy-start | bytes 28
  6.5 15.9 %copy-start.10 = (s32[256,8,3]{0,1,2:T(8,128)S(1)}, s32[256,8,3]{0,1,2:T(8,128)}, u32[]{:S(2)}) copy-start(s32[256,8,3]{0,1,2:T(8,128)} %param.24) | copy-start | bytes 73732
  6.5 452.1 %all-gather.5.cloned.1.call-start = ((), (), s32[]{:S(2)}) async-start(), calls=%async_computation.3 | async-start | bytes 8912896 | tf_op jit(solution)/shard_map/all_gather | solution.py:40
  8.1 25.0 %copy-start.2 = (bf16[1024,512]{0,1:T(8,128)(2,1)}, bf16[1024,512]{0,1:T(8,128)(2,1)S(1)}, u32[]{:S(2)}) copy-start(bf16[1024,512]{0,1:T(8,128)(2,1)S(1)} %copy.129) | copy-start | bytes 3145732
  10.0 24.8 %copy-start.3 = (bf16[1024,512]{0,1:T(8,128)(2,1)}, bf16[1024,512]{0,1:T(8,128)(2,1)S(1)}, u32[]{:S(2)}) copy-start(bf16[1024,512]{0,1:T(8,128)(2,1)S(1)} %copy.130) | copy-start | bytes 3145732
  11.1 27.1 %collective-permute-start.1 = (bf16[64,8,128]{0,2,1:T(8,128)(2,1)}, bf16[64,8,128]{0,2,1:T(8,128)(2,1)}, u32[]{:S(2)}, u32[]{:S(2)}) collective-permute-start(bf16[64,8,128]{0,2,1:T(8,128)(2,1)} %get-tuple-element.243), channel_id=1, source_target_pairs={{2,0},{4,2},{6,4},{8,6},{10,8},{12,10},{14,12},{16,14},{18,16},{20... | collective-permute-start | bytes 393224 | tf_op jit(solution)/shard_map/ppermute | solution.py:24
  15.1 23.1 %collective-permute-start = (bf16[64,8,128]{0,2,1:T(8,128)(2,1)}, bf16[64,8,128]{0,2,1:T(8,128)(2,1)}, u32[]{:S(2)}, u32[]{:S(2)}) collective-permute-start(bf16[64,8,128]{0,2,1:T(8,128)(2,1)} %get-tuple-element.244), channel_id=1, source_target_pairs={{0,2},{2,4},{4,6},{6,8},{8,10},{10,12},{12,14},{14,16},{16,18},{18... | collective-permute-start | bytes 393224 | tf_op jit(solution)/shard_map/ppermute | solution.py:21
  34.9 3.3 copy-start.20
  80.4 135.3 %collective-permute-start.2 = (bf16[8,24,64,128]{3,2,1,0:T(8,128)(2,1)}, bf16[8,24,64,128]{3,2,1,0:T(8,128)(2,1)}, u32[]{:S(2)}, u32[]{:S(2)}) collective-permute-start(bf16[8,24,64,128]{3,2,1,0:T(8,128)(2,1)} %gather_fusion.4), channel_id=1, source_target_pairs={{0,2},{2,0},{4,6},{6,4},{8,10},{10,8},{12,14},{14,12},{16,18},{18,... | collective-permute-start | bytes 9437192 | tf_op jit(solution)/shard_map/ppermute | solution.py:36
  209.5 4.2 copy-start.4
  211.7 2.0 copy-start.1
  211.7 3.9 copy-start.19
  215.4 541.8 %all-reduce.4.cloned.1.call-start = ((), (), s32[]{:S(2)}) async-start(), calls=%async_computation.1 | async-start | bytes 8388608 | tf_op jit(solution)/shard_map/psum | solution.py:203
  225.5 13.5 %copy-start.18 = (s32[8]{0:T(128)S(1)}, s32[8]{0:T(128)}, u32[]{:S(2)}) copy-start(s32[8]{0:T(128)} %constant.281.clone) | copy-start | bytes 100
  230.9 67.7 %collective-permute-start.3 = (bf16[8,24,64,128]{3,2,1,0:T(8,128)(2,1)}, bf16[8,24,64,128]{3,2,1,0:T(8,128)(2,1)}, u32[]{:S(2)}, u32[]{:S(2)}) collective-permute-start(bf16[8,24,64,128]{3,2,1,0:T(8,128)(2,1)} %gather_fusion.5), channel_id=1, source_target_pairs={{0,4},{4,0},{2,6},{6,2},{8,12},{12,8},{10,14},{14,10},{16,20},{20,... | collective-permute-start | bytes 9437192 | tf_op jit(solution)/shard_map/ppermute | solution.py:36
  308.8 29.5 %copy-start.8 = (bf16[2,1,64,512]{3,2,1,0:T(8,128)(2,1)S(1)}, bf16[2,1,64,512]{3,2,1,0:T(8,128)(2,1)}, u32[]{:S(2)}) copy-start(bf16[2,1,64,512]{3,2,1,0:T(8,128)(2,1)} %get-tuple-element.247) | copy-start | bytes 393220
  314.4 145.4 %collective-permute-start.4 = (bf16[8,24,64,128]{3,2,1,0:T(8,128)(2,1)}, bf16[8,24,64,128]{3,2,1,0:T(8,128)(2,1)}, u32[]{:S(2)}, u32[]{:S(2)}) collective-permute-start(bf16[8,24,64,128]{3,2,1,0:T(8,128)(2,1)} %gather_fusion.6), channel_id=1, source_target_pairs={{0,8},{8,0},{2,10},{10,2},{4,12},{12,4},{6,14},{14,6},{16,24},{24,... | collective-permute-start | bytes 9437192 | tf_op jit(solution)/shard_map/ppermute | solution.py:36
  330.9 12.5 %copy-start.12 = (s32[384]{0:T(512)}, s32[384]{0:T(512)S(1)}, u32[]{:S(2)}) copy-start(s32[384]{0:T(512)S(1)} %fusion.70) | copy-start | bytes 4612
  339.2 111.2 %copy-start.7 = (bf16[2,64,8,64]{3,1,0,2:T(8,128)(2,1)S(1)}, bf16[2,64,8,64]{3,1,0,2:T(8,128)(2,1)}, u32[]{:S(2)}) copy-start(bf16[2,64,8,64]{3,1,0,2:T(8,128)(2,1)} %copy.152) | copy-start | bytes 393220
  339.3 112.1 %copy-start.15 = (pred[16,1]{1,0:T(8,128)(4,1)S(1)}, pred[16,1]{1,0:T(8,128)(4,1)}, u32[]{:S(2)}) copy-start(pred[16,1]{1,0:T(8,128)(4,1)} %copy.156) | copy-start | bytes 52
  339.3 112.1 %copy-start.16 = (pred[16,1]{1,0:T(8,128)(4,1)S(1)}, pred[16,1]{1,0:T(8,128)(4,1)}, u32[]{:S(2)}) copy-start(pred[16,1]{1,0:T(8,128)(4,1)} %copy.155) | copy-start | bytes 52
  446.1 0.7 copy-start.9
  475.5 142.1 %collective-permute-start.5 = (bf16[8,24,64,128]{3,2,1,0:T(8,128)(2,1)}, bf16[8,24,64,128]{3,2,1,0:T(8,128)(2,1)}, u32[]{:S(2)}, u32[]{:S(2)}) collective-permute-start(bf16[8,24,64,128]{3,2,1,0:T(8,128)(2,1)} %gather_fusion.7), channel_id=1, source_target_pairs={{0,16},{16,0},{2,18},{18,2},{4,20},{20,4},{6,22},{22,6},{8,24},{24... | collective-permute-start | bytes 9437192 | tf_op jit(solution)/shard_map/ppermute | solution.py:36
  487.4 130.2 %copy-start.17 = (s32[8]{0:T(128)S(1)}, s32[8]{0:T(128)}, u32[]{:S(2)}) copy-start(s32[8]{0:T(128)} %constant.282.clone) | copy-start | bytes 100
  627.4 6.8 copy-start.22
  634.2 6.0 copy-start.13
  640.2 6.8 copy-start.11
  647.1 7.1 copy-start.6
  654.2 3.0 copy-start.5
  654.2 3.0 copy-start.14
  725.0 36.4 %copy-start.23 = (f32[1024]{0:T(1024)S(1)}, f32[1024]{0:T(1024)}, u32[]{:S(2)}) copy-start(f32[1024]{0:T(1024)} %param.27) | copy-start | bytes 12292
  725.0 64.2 %reduce-scatter.2.cloned.1.call-start = ((), (), s32[]{:S(2)}) async-start(), calls=%async_computation.2 | async-start | bytes 6291456 | tf_op jit(solution)/shard_map/reduce_scatter | solution.py:215
Sparse Core Ops, SparseCore 0:
  215.5 160.5 all-gather.4
  725.1 32.0 all-reduce.3
  776.0 13.1 reduce-scatter.1
where the time goes:
time: 812 us; the launch traced here: 799 us
  blocking collectives  227 us (28%)
  waiting for transfers between devices  200 us (25%)
  local copies, waits for them, and re-layouts  154 us (19%)
  other arithmetic  108 us (13%)
  matrix products  62.7 us (8%)
  starting transfers between devices  28.7 us (4%)
  between operations  18.8 us (2%)
    ppermute x4, waiting for transfers between devices, swapped(): return lax.ppermute(block, axis, route)  154 us
    psum x1, blocking collectives, local(): summed_rows = lax.psum(jnp.stack(contributions, axis=0), 'seq')  124 us
    all_gather x2, blocking collectives, joined(): everything = jax.tree.map(lambda part: lax.all_gather(part, axis), shard)  103 us
    scatter x4, local copies, waits for them, and re-layouts, local(): buffer_rows = buffer_rows.at[moving].set(inbound)  40.1 us
    psum x1, waiting for transfers between devices, local(): attn_full = lax.psum(projected, 'mp')  32.2 us
    add x15, other arithmetic, combine_parts(): accum_a * factor_a[..., None] + accum_b * factor_b[..., None]  23.3 us
    ppermute x4, starting transfers between devices, swapped(): return lax.ppermute(block, axis, route)  22.5 us
    gather x4, local copies, waits for them, and re-layouts, local(): outbound = jnp.take(buffer_rows, moving, axis=0)  21.8 us
  transfers between devices with their start and end apart: 9, of which 4 were waited for; matrix products, arithmetic and copies ran while one was open for 16% of the time, Pallas kernels for 0%

commit v1 on v0

v1 whole, which is shorter than its diff:
```python
import functools

import jax
import jax.numpy as jnp
from jax import lax
from jax.experimental import pallas as pl
from jax.experimental.pallas import tpu as pltpu
from jax.sharding import PartitionSpec as P

HD = 64
BLK = 64
R = 3
GLOB = 2
GROUP = 16
QB_DEV = 16
VMEM_LIMIT = 56 * 1024 * 1024
NT = (((1,), (1,)), ((), ()))


def half_mask(rows):
    return lax.broadcasted_iota(jnp.int32, (rows, 2 * HD), 1) < HD


def pack_kernel(index_ref, key_ref, value_ref, out_ref, tiles_ref):
    pairs = key_ref.shape[1] // (2 * HD)
    low = half_mask(BLK)

    def build(block, carry):
        rows = pl.ds(pl.multiple_of(block * BLK, BLK), BLK)
        for pair in range(pairs):
            cols = slice(pair * 2 * HD, (pair + 1) * 2 * HD)
            keys = key_ref[rows, cols].astype(jnp.float32)
            turned = pltpu.roll(value_ref[rows, cols].astype(jnp.float32), HD, 1)
            at = block * (2 * pairs) + 2 * pair
            tiles_ref[at] = jnp.where(low, keys, turned).astype(jnp.bfloat16)
            tiles_ref[at + 1] = jnp.where(low, turned, keys).astype(jnp.bfloat16)
        return carry

    lax.fori_loop(0, QB_DEV, build, 0)

    def pick(step, carry):
        for inner in range(8):
            slot = step * 8 + inner
            out_ref[slot] = tiles_ref[index_ref[slot]]
        return carry

    lax.fori_loop(0, out_ref.shape[0] // 8, pick, 0)


def pack(chosen, key_rows, value_rows):
    slots = chosen.shape[0]
    heads_here = key_rows.shape[1] // HD
    return pl.pallas_call(
        pack_kernel,
        out_shape=jax.ShapeDtypeStruct((slots, BLK, 2 * HD), jnp.bfloat16),
        in_specs=[
            pl.BlockSpec(memory_space=pltpu.SMEM),
            pl.BlockSpec(memory_space=pltpu.VMEM),
            pl.BlockSpec(memory_space=pltpu.VMEM),
        ],
        out_specs=pl.BlockSpec(memory_space=pltpu.VMEM),
        scratch_shapes=[pltpu.VMEM((QB_DEV * heads_here, BLK, 2 * HD), jnp.bfloat16)],
        compiler_params=pltpu.CompilerParams(vmem_limit_bytes=VMEM_LIMIT),
        name="pack",
    )(chosen, key_rows, value_rows)


def attend_kernel(
    slot_ref, first_ref, q_ref, k_ref, v_ref, gk_ref, gv_ref, rand_ref, out_ref
):
    block = pl.program_id(0)
    pairs = q_ref.shape[1] // (2 * HD)
    heads_here = 2 * pairs
    low = half_mask(BLK)
    rows = pl.ds(pl.multiple_of(block * BLK, BLK), 3 * BLK)
    cut_low = jnp.where((block == 0) & (first_ref[0] == 1), -1e30, 0.0)
    cut_high = jnp.where((block == QB_DEV - 1) & (first_ref[1] == 1), -1e30, 0.0)
    zeros = jnp.zeros((BLK, 2 * HD), jnp.bfloat16)
    for pair in range(pairs):
        cols = slice(pair * 2 * HD, (pair + 1) * 2 * HD)
        query = q_ref[:, cols] * jnp.bfloat16(HD**-0.5)
        q_even = jnp.where(low, query, zeros)
        q_odd = jnp.where(low, zeros, query)
        stacked = jnp.concatenate([q_even, q_odd], axis=0)
        spread = jnp.concatenate(
            [
                jnp.concatenate([q_even, zeros], axis=1),
                jnp.concatenate([zeros, q_odd], axis=1),
            ],
            axis=0,
        )
        random_tiles = []
        for r in range(R):
            at = (block * heads_here + 2 * pair) * R + r
            random_tiles.append(
                jnp.concatenate(
                    [rand_ref[slot_ref[at]], rand_ref[slot_ref[at + R]]], axis=1
                )
            )
        random_kv = jnp.concatenate(random_tiles, axis=0)
        keys = jnp.concatenate([k_ref[rows, cols], gk_ref[:, cols]], axis=0)
        values = jnp.concatenate([v_ref[rows, cols], gv_ref[:, cols]], axis=0)
        near = lax.dot_general(keys, stacked, NT, preferred_element_type=jnp.float32)
        far = lax.dot_general(random_kv, spread, NT, preferred_element_type=jnp.float32)
        near = jnp.concatenate(
            [near[:BLK] + cut_low, near[BLK : 2 * BLK], near[2 * BLK : 3 * BLK] + cut_high, near[3 * BLK :]],
            axis=0,
        )
        peak = jnp.maximum(
            jnp.max(near, axis=0, keepdims=True), jnp.max(far, axis=0, keepdims=True)
        )
        near = jnp.exp(near - peak)
        far = jnp.exp(far - peak)
        total = jnp.sum(near, axis=0, keepdims=True) + jnp.sum(far, axis=0, keepdims=True)
        contract = (((0,), (0,)), ((), ()))
        near_out = lax.dot_general(
            values, near.astype(jnp.bfloat16), contract, preferred_element_type=jnp.float32
        )
        far_out = lax.dot_general(
            random_kv, far.astype(jnp.bfloat16), contract, preferred_element_type=jnp.float32
        )
        even = near_out[:HD] + far_out[HD : 2 * HD]
        odd = near_out[HD:] + far_out[2 * HD : 3 * HD]
        lanes = lax.broadcasted_iota(jnp.int32, (HD, 2 * BLK), 1) < BLK
        both = jnp.concatenate([jnp.where(lanes, even, 0.0), jnp.where(lanes, 0.0, odd)], axis=0)
        both = (both / total).T
        out_ref[:, cols] = (both[:BLK] + both[BLK:]).astype(jnp.bfloat16)


def attend(slots, edges, query_rows, keys, values, global_k, global_v, received):
    tokens, width = query_rows.shape

    def whole(array):
        return pl.BlockSpec(array.shape, lambda i, *_: (0,) * array.ndim)

    return pl.pallas_call(
        attend_kernel,
        out_shape=jax.ShapeDtypeStruct((tokens, width), jnp.bfloat16),
        grid_spec=pltpu.PrefetchScalarGridSpec(
            num_scalar_prefetch=2,
            grid=(QB_DEV,),
            in_specs=[
                pl.BlockSpec((BLK, width), lambda i, *_: (i, 0)),
                whole(keys),
                whole(values),
                whole(global_k),
                whole(global_v),
                whole(received),
            ],
            out_specs=pl.BlockSpec((BLK, width), lambda i, *_: (i, 0)),
        ),
        compiler_params=pltpu.CompilerParams(vmem_limit_bytes=VMEM_LIMIT),
        name="attend",
    )(slots, edges, query_rows, keys, values, global_k, global_v, received)


def local(
    residual_in,
    query_rows,
    key_rows,
    value_rows,
    rand_blocks,
    global_blocks,
    out_weight,
    norm_gain,
    up_weight,
    down_weight,
):
    tok_rows, local_width = query_rows.shape
    heads_here = local_width // HD
    shard_count = lax.axis_size("seq")
    my_shard = lax.axis_index("seq")
    mp_index = lax.axis_index("mp")
    other = 1 - mp_index
    swap = [(0, 1), (1, 0)]
    score_scale = HD**-0.5
    position = my_shard % GROUP
    group_base = my_shard - position
    slot_count = QB_DEV * heads_here * R
    capacity = slot_count // GROUP

    wanted = lax.dynamic_slice_in_dim(
        rand_blocks, group_base * QB_DEV, GROUP * QB_DEV, 0
    ).reshape(GROUP, slot_count)
    counting = jnp.arange(slot_count, dtype=jnp.int32)
    earlier = (counting[:, None] < counting[None, :]).astype(jnp.bfloat16)
    slot_heads = counting // R % heads_here
    from_me = wanted // QB_DEV == my_shard
    my_requests = lax.dynamic_index_in_dim(wanted, position, 0, keepdims=False)
    owner = my_requests // QB_DEV - group_base
    by_owner = owner[None, :] == jnp.arange(GROUP, dtype=jnp.int32)[:, None]
    ranks = jnp.dot(
        jnp.concatenate([from_me, by_owner], axis=0).astype(jnp.bfloat16),
        earlier,
        preferred_element_type=jnp.float32,
    ).astype(jnp.int32)
    source = wanted % QB_DEV * heads_here + slot_heads[None, :]
    pick_table = from_me[:, None, :] & (
        ranks[:GROUP, None, :] == jnp.arange(capacity, dtype=jnp.int32)[None, :, None]
    )
    chosen = jnp.sum(jnp.where(pick_table, source[:, None, :], 0), axis=2)
    my_rank = jnp.sum(jnp.where(by_owner, ranks[GROUP:], 0), axis=0)
    slots = owner * capacity + my_rank

    sections = pack(chosen.reshape(slot_count), key_rows, value_rows)
    groups = [
        list(range(start, start + GROUP)) for start in range(0, shard_count, GROUP)
    ]
    received = lax.all_to_all(
        sections, "seq", 0, 0, axis_index_groups=groups, tiled=True
    )

    other_out = lax.ppermute(out_weight, "mp", swap)
    other_up = lax.ppermute(up_weight, "mp", swap)
    other_down = lax.ppermute(down_weight, "mp", swap)

    both = jnp.stack([key_rows, value_rows], axis=0)
    forward = [(i, i + 1) for i in range(shard_count - 1)]
    backward = [(i + 1, i) for i in range(shard_count - 1)]
    below = lax.ppermute(both[:, tok_rows - BLK :], "seq", forward)
    above = lax.ppermute(both[:, :BLK], "seq", backward)
    padded = jnp.concatenate([below, both, above], axis=1)

    packed = jnp.stack([query_rows, key_rows, value_rows], axis=0)
    contributions = []
    for which in range(GLOB):
        global_id = global_blocks[which]
        block_rows = lax.dynamic_slice_in_dim(packed, global_id % QB_DEV * BLK, BLK, 1)
        is_owner = global_id // QB_DEV == my_shard
        contributions.append(jnp.where(is_owner, block_rows, jnp.zeros_like(block_rows)))
    global_qkv = lax.psum(jnp.concatenate(contributions, axis=1), "seq")
    global_q = global_qkv[0].reshape(GLOB * BLK, heads_here, HD)
    global_k, global_v = global_qkv[1], global_qkv[2]

    key_heads = key_rows.reshape(tok_rows, heads_here, HD)
    value_heads = value_rows.reshape(tok_rows, heads_here, HD)
    global_scores = (
        jnp.einsum("qhd,thd->hqt", global_q, key_heads, preferred_element_type=jnp.float32)
        * score_scale
    )
    seg_peak = jnp.max(global_scores, axis=2)
    seg_weights = jnp.exp(global_scores - seg_peak[..., None])
    seg_total = jnp.sum(seg_weights, axis=2)
    seg_acc = jnp.einsum(
        "hqt,thd->hqd",
        seg_weights.astype(jnp.bfloat16),
        value_heads,
        preferred_element_type=jnp.float32,
    )
    stats = lax.all_gather(jnp.stack([seg_peak, seg_total], axis=0), "seq")
    top = jnp.max(stats[:, 0], axis=0)
    merged_total = jnp.sum(jnp.exp(stats[:, 0] - top) * stats[:, 1], axis=0)
    factor = jnp.exp(seg_peak - top) / merged_total
    global_out = lax.psum(seg_acc * factor[..., None], "seq")
    global_rows = (
        global_out.transpose(1, 0, 2).reshape(GLOB * BLK, local_width).astype(jnp.bfloat16)
    )

    edges = jnp.stack([my_shard == 0, my_shard == shard_count - 1]).astype(jnp.int32)
    attention = attend(
        slots, edges, query_rows, padded[0], padded[1], global_k, global_v, received
    )
    for which in range(GLOB):
        global_id = global_blocks[which]
        start_row = global_id % QB_DEV * BLK
        current = lax.dynamic_slice_in_dim(attention, start_row, BLK, 0)
        replacing = global_rows[which * BLK : (which + 1) * BLK]
        is_owner = global_id // QB_DEV == my_shard
        attention = lax.dynamic_update_slice_in_dim(
            attention, jnp.where(is_owner, replacing, current), start_row, 0
        )

    half_rows = tok_rows // 2
    half_width = residual_in.shape[1] // 2
    own_heads = lax.dynamic_slice_in_dim(attention, mp_index * half_rows, half_rows, 0)
    other_heads = lax.ppermute(
        lax.dynamic_slice_in_dim(attention, other * half_rows, half_rows, 0), "mp", swap
    )
    residual = lax.dynamic_slice_in_dim(residual_in, mp_index * half_rows, half_rows, 0)
    projected = jnp.dot(own_heads, out_weight, preferred_element_type=jnp.float32) + jnp.dot(
        other_heads, other_out, preferred_element_type=jnp.float32
    )
    middle = (residual.astype(jnp.float32) + projected).astype(jnp.bfloat16)
    middle32 = middle.astype(jnp.float32)
    row_mean = jnp.mean(middle32, axis=1, keepdims=True)
    centered = middle32 - row_mean
    row_var = jnp.mean(centered * centered, axis=1, keepdims=True)
    normed = (centered * lax.rsqrt(row_var + 1e-05) * norm_gain).astype(jnp.bfloat16)
    total = middle32
    for up, down in ((up_weight, down_weight), (other_up, other_down)):
        hidden = jax.nn.gelu(
            jnp.dot(normed, up, preferred_element_type=jnp.float32), approximate=True
        ).astype(jnp.bfloat16)
        total = total + jnp.dot(hidden, down, preferred_element_type=jnp.float32)
    result = total.astype(jnp.bfloat16)
    own_part = lax.dynamic_slice_in_dim(result, mp_index * half_width, half_width, 1)
    other_part = lax.ppermute(
        lax.dynamic_slice_in_dim(result, other * half_width, half_width, 1), "mp", swap
    )
    first = mp_index == 0
    return jnp.concatenate(
        [jnp.where(first, own_part, other_part), jnp.where(first, other_part, own_part)], axis=0
    )


def solution(mesh):
    placed = (
        P("seq", None),
        P("seq", "mp"),
        P("seq", "mp"),
        P("seq", "mp"),
        P(None, "mp", None),
        P(),
        P("mp", None),
        P(),
        P(None, "mp"),
        P("mp", None),
    )
    return jax.shard_map(
        local, mesh=mesh, in_specs=placed, out_specs=P("seq", "mp"), check_vma=False
    )
```

time: 812 us -> 420 us (0.52)
  the two profiles are of different devices: /device:TPU:17 before, /device:TPU:0 now
where the time goes in v1:
time: 420 us; the launch traced here: 419 us
  waiting for transfers between devices  191 us (45%)
  blocking collectives  114 us (27%)
  Pallas kernels  35.8 us (9%)
  matrix products  25.8 us (6%)
  between operations  18.8 us (4%)
  starting transfers between devices  15 us (4%)
  other arithmetic  9.75 us (2%)
  local copies, waits for them, and re-layouts  9.65 us (2%)
    psum x1, waiting for transfers between devices, local(): global_qkv = lax.psum(jnp.concatenate(contributions, axis=1), 'seq')  179 us
    psum x1, blocking collectives, local(): global_out = lax.psum(seg_acc * factor[..., None], 'seq')  74.4 us
    all_gather x1, blocking collectives, local(): stats = lax.all_gather(jnp.stack([seg_peak, seg_total], axis=0), 'seq')  39.5 us
    pallas_call x1, Pallas kernels, attend(): pl.pallas_call(attend_kernel, out_shape=jax.ShapeDtypeStruct((tokens, wid...  29.5 us
    dot_general x2, matrix products, local(): total = total + jnp.dot(hidden, down, preferred_element_type=jnp.float32)  18.2 us
    ppermute x1, waiting for transfers between devices, local(): below = lax.ppermute(both[:, tok_rows - BLK:], 'seq', forward)  9.29 us
    all_to_all x1, starting transfers between devices, local(): lax.all_to_all(sections, 'seq', 0, 0, axis_index_groups=groups, tiled=True)  8.63 us
  transfers between devices with their start and end apart: 9, of which 4 were waited for; matrix products, arithmetic and copies ran while one was open for 8% of the time, Pallas kernels for 7%

profile of v1, /device:TPU:0, one launch (start us, length us, event | category | flops | bytes accessed | tf_op | source)
XLA Modules:
  0.0 419.3 jit_solution(4242368956825374239)
XLA Ops:
  6.6 1.2 copy.32
  7.7 0.5 reshape.128
  8.3 0.2 convolution_convert_fusion
  8.5 0.4 select_reduce_fusion
  8.9 0.7 reshape.129.index_ref
  9.5 6.3 %pack.1 = bf16[384,64,128]{2,1,0:T(8,128)(2,1)} custom-call(s32[384]{0:T(512)} %reshape.129.index_ref, bf16[1024,512]{1,0:T(8,128)(2,1)} %key_ref.1, bf16[1024,512]{1,0:T(8,128)(2,1)} %value_ref.1), custom_call_target="tpu_custom_call" | custom-call | tf_op jit(solution)/shard_map/pack/pallas_call | solution.py:53
  15.9 8.6 %all-to-all-start = ((bf16[384,64,128]{2,1,0:T(8,128)(2,1)}), bf16[384,64,128]{2,1,0:T(8,128)(2,1)}, u32[]{:S(2)}, u32[]{:S(2)}) async-start(bf16[384,64,128]{2,1,0:T(8,128)(2,1)} %pack.1), calls=%async_computation | async-start | bytes 12582912 | tf_op jit(solution)/shard_map/all_to_all | solution.py:209
  24.6 0.6 fusion.97
  30.3 0.3 pad_maximum_fusion
  30.6 0.1 dynamic-slice_select_fusion.1
  30.7 0.8 pad_maximum_fusion.3
  31.6 3.8 collective-permute-start
  35.4 1.3 collective-permute-start.1
  36.7 0.1 collective-permute-start.3
  36.7 0.5 collective-permute-start.4
  37.2 0.1 collective-permute-start.5
  37.3 0.6 fusion.65.slot_ref
  37.9 1.3 copy.34
  39.2 0.5 copy.35
  39.8 0.6 add_convert_fusion.1.first_ref
  40.3 9.3 %collective-permute-done = bf16[2,64,512]{2,1,0:T(8,128)(2,1)S(1)} collective-permute-done((bf16[2,64,512]{2,1,0:T(8,128)(2,1)S(1)}, bf16[2,64,512]{2,1,0:T(8,128)(2,1)S(1)}, u32[]{:S(2)}, u32[]{:S(2)}) %collective-permute-start) | collective-permute-done | bytes 131104 | tf_op jit(solution)/shard_map/ppermute | solution.py:220
  49.6 0.8 collective-permute-done.1
  50.4 1.1 pad_maximum_fusion.1
  51.5 1.6 slice_bitcast_fusion
  53.0 178.9 %all-reduce.3.cloned.1.call-done = bf16[3,128,512]{2,1,0:T(8,128)(2,1)} async-done(((bf16[3,128,512]{2,1,0:T(8,128)(2,1)}), bf16[3,128,512]{2,1,0:T(8,128)(2,1)}) %all-reduce.3.cloned.1.call-update) | async-done | bytes 393232 | tf_op jit(solution)/shard_map/psum | solution.py:231
  232.0 1.8 fusion.94
  233.7 0.1 copy.33
  233.9 2.1 multiply_reduce_fusion
  235.9 0.9 fusion.16
  236.8 39.5 %all-gather = f32[32,8,128]{2,1,0:T(8,128)S(1)} all-gather(f32[2,8,128]{2,1,0:T(8,128)S(1)} %pad_maximum_fusion.6), channel_id=2, replica_groups=mesh['seq'=16,'mp'=2] {'seq'}, dimensions={0}, use_global_device_ids=true | all-gather | bytes 139264 | tf_op jit(solution)/shard_map/all_gather | solution.py:250
  276.4 1.0 fusion.43
  277.4 74.4 %all-reduce.4 = bf16[8,128,64]{1,2,0:T(8,128)(2,1)S(1)} all-reduce(f32[8,128,64]{1,2,0:T(8,128)S(1)} %fusion.43), channel_id=1, replica_groups=mesh['seq'=16,'mp'=2] {'seq'}, use_global_device_ids=true, to_apply=%region_7.8 | all-reduce | flops 65536 | bytes 393216 | tf_op jit(solution)/shard_map/psum | solution.py:254
  351.8 0.1 fusion.95
  351.9 0.1 copy.39
  352.0 0.1 copy.40
  352.1 29.5 %attend.1 = bf16[1024,512]{1,0:T(8,128)(2,1)} custom-call(s32[384]{0:T(512)} %fusion.65.slot_ref, s32[2]{0:T(128)} %add_convert_fusion.1.first_ref, bf16[1024,512]{1,0:T(8,128)(2,1)} %q_ref.1, bf16[1152,512]{1,0:T(8,128)(2,1)} %get-tuple-element.10.k_ref, bf16[1152,512]{1,0:T(8,128)(2,1)} %get-tuple-element.9.v_ref, ...), custom_call_target="tpu_custom_call" | custom-call | tf_op jit(solution)/shard_map/attend/pallas_call | solution.py:136
  381.7 1.6 select_dynamic-update-slice_fusion.1
  383.3 1.5 select_dynamic-update-slice_fusion
  384.8 1.1 constant_dynamic-slice_fusion.1
  385.9 2.1 fusion.47
  388.1 2.3 convert_reduce_fusion
  390.4 0.4 fusion.20
  390.8 9.5 %fusion.29 = f32[512,1024]{1,0:T(8,128)} fusion(bf16[2048,1024]{1,0:T(8,128)(2,1)} %param.19, bf16[1024,2048]{1,0:T(8,128)(2,1)} %param.18, bf16[512,1024]{1,0:T(8,128)(2,1)S(1)} %get-tuple-element.27, f32[1024]{0:T(1024)S(1)} %copy-done.5, f32[512]{0:T(512)S(1)} %add_rsqrt_fusion, f32[512]{0:T(512)S(1)} %broadcast_multiply_fusion), kind=kOutput, calls=%fused_computation.36 | convolution fusion | flops 4307025920 | bytes 11542528 | tf_op jit(solution)/shard_map/dot_general | solution.py:294
  400.3 8.7 %fusion.24 = bf16[512,1024]{1,0:T(8,128)(2,1)S(1)} fusion(f32[512,1024]{1,0:T(8,128)} %fusion.29, bf16[512,1024]{1,0:T(8,128)(2,1)S(1)} %get-tuple-element.27, bf16[2048,1024]{1,0:T(8,128)(2,1)} %collective-permute-done.5, bf16[1024,2048]{1,0:T(8,128)(2,1)} %collective-permute-done.4, f32[1024]{0:T(1024)S(1)} %copy-done.5, f32[512]{0:T(512)S(1)} %add_rsqrt_fusion, ...), kind=kOutput, calls=%fused_computation.33 | convolution fusion | flops 4309123072 | bytes 12591104 | tf_op jit(solution)/shard_map/dot_general | solution.py:294
  409.1 0.6 collective-permute-start.6
  409.6 1.5 collective-permute-done.6
  411.2 0.2 broadcast_select_fusion.1
  411.4 1.0 pad_maximum_fusion.2
  (33 shorter events, 0.4 us)
Async XLA Ops:
  15.9 8.7 %copy-start.4 = (s32[2]{0:T(128)S(1)}, s32[2]{0:T(128)}, u32[]{:S(2)}) copy-start(s32[2]{0:T(128)} %param.15) | copy-start | bytes 28
  15.9 14.4 %copy-start = (bf16[1024,512]{1,0:T(8,128)(2,1)S(1)}, bf16[1024,512]{1,0:T(8,128)(2,1)}, u32[]{:S(2)}) copy-start(bf16[1024,512]{1,0:T(8,128)(2,1)} %value_ref.1) | copy-start | bytes 3145732
  15.9 14.4 %copy-start.1 = (bf16[1024,512]{1,0:T(8,128)(2,1)S(1)}, bf16[1024,512]{1,0:T(8,128)(2,1)}, u32[]{:S(2)}) copy-start(bf16[1024,512]{1,0:T(8,128)(2,1)} %key_ref.1) | copy-start | bytes 3145732
  15.9 14.4 %copy-start.2 = (bf16[1024,512]{1,0:T(8,128)(2,1)S(1)}, bf16[1024,512]{1,0:T(8,128)(2,1)}, u32[]{:S(2)}) copy-start(bf16[1024,512]{1,0:T(8,128)(2,1)} %q_ref.1) | copy-start | bytes 3145732
  15.9 336.3 %all-to-all-start = ((bf16[384,64,128]{2,1,0:T(8,128)(2,1)}), bf16[384,64,128]{2,1,0:T(8,128)(2,1)}, u32[]{:S(2)}, u32[]{:S(2)}) async-start(bf16[384,64,128]{2,1,0:T(8,128)(2,1)} %pack.1), calls=%async_computation | async-start | bytes 12582912 | tf_op jit(solution)/shard_map/all_to_all | solution.py:209
  24.5 207.5 %all-reduce.3.cloned.1.call-start = ((), (), s32[]{:S(2)}) async-start(), calls=%async_computation.1 | async-start | bytes 786432 | tf_op jit(solution)/shard_map/psum | solution.py:231
  31.6 18.1 %collective-permute-start = (bf16[2,64,512]{2,1,0:T(8,128)(2,1)S(1)}, bf16[2,64,512]{2,1,0:T(8,128)(2,1)S(1)}, u32[]{:S(2)}, u32[]{:S(2)}) collective-permute-start(bf16[2,64,512]{2,1,0:T(8,128)(2,1)S(1)} %get-tuple-element.11), channel_id=1, source_target_pairs={{0,2},{2,4},{4,6},{6,8},{8,10},{10,12},{12,14},{14,16},{16,18},{18... | collective-permute-start | bytes 393224 | tf_op jit(solution)/shard_map/ppermute | solution.py:220
  35.4 15.0 %collective-permute-start.1 = (bf16[2,64,512]{2,1,0:T(8,128)(2,1)S(1)}, bf16[2,64,512]{2,1,0:T(8,128)(2,1)}, u32[]{:S(2)}, u32[]{:S(2)}) collective-permute-start(bf16[2,64,512]{2,1,0:T(8,128)(2,1)S(1)} %get-tuple-element.12), channel_id=1, source_target_pairs={{2,0},{4,2},{6,4},{8,6},{10,8},{12,10},{14,12},{16,14},{18,16},{20... | collective-permute-start | bytes 393224 | tf_op jit(solution)/shard_map/ppermute | solution.py:221
  36.7 351.4 %collective-permute-start.3 = (bf16[512,1024]{1,0:T(8,128)(2,1)}, bf16[512,1024]{1,0:T(8,128)(2,1)}, u32[]{:S(2)}, u32[]{:S(2)}) collective-permute-start(bf16[512,1024]{1,0:T(8,128)(2,1)} %param.16), channel_id=1, source_target_pairs={{0,1},{1,0},{2,3},{3,2},{4,5},{5,4},{6,7},{7,6},{8,9},{9,8},{10,11... | collective-permute-start | bytes 3145736 | tf_op jit(solution)/shard_map/ppermute | solution.py:213
  36.7 363.6 %collective-permute-start.4 = (bf16[1024,2048]{1,0:T(8,128)(2,1)}, bf16[1024,2048]{1,0:T(8,128)(2,1)}, u32[]{:S(2)}, u32[]{:S(2)}) collective-permute-start(bf16[1024,2048]{1,0:T(8,128)(2,1)} %param.18), channel_id=1, source_target_pairs={{0,1},{1,0},{2,3},{3,2},{4,5},{5,4},{6,7},{7,6},{8,9},{9,8},{10,11... | collective-permute-start | bytes 12582920 | tf_op jit(solution)/shard_map/ppermute | solution.py:214
  37.2 363.1 %collective-permute-start.5 = (bf16[2048,1024]{1,0:T(8,128)(2,1)}, bf16[2048,1024]{1,0:T(8,128)(2,1)}, u32[]{:S(2)}, u32[]{:S(2)}) collective-permute-start(bf16[2048,1024]{1,0:T(8,128)(2,1)} %param.19), channel_id=1, source_target_pairs={{0,1},{1,0},{2,3},{3,2},{4,5},{5,4},{6,7},{7,6},{8,9},{9,8},{10,11... | collective-permute-start | bytes 12582920 | tf_op jit(solution)/shard_map/ppermute | solution.py:215
  381.7 6.4 %copy-start.3 = (bf16[1024,1024]{1,0:T(8,128)(2,1)S(1)}, bf16[1024,1024]{1,0:T(8,128)(2,1)}, u32[]{:S(2)}) copy-start(bf16[1024,1024]{1,0:T(8,128)(2,1)} %param.10) | copy-start | bytes 6291460
  385.9 2.2 collective-permute-start.2
  388.0 2.8 copy-start.5
  409.1 2.1 collective-permute-start.6
Sparse Core Ops, SparseCore 0:
  31.7 200.2 all-reduce.2

commit v2 on v1

--- a/solution.py
+++ b/solution.py
@@ -15,6 +15,7 @@
 QB_DEV = 16
 VMEM_LIMIT = 56 * 1024 * 1024
 NT = (((1,), (1,)), ((), ()))
+TT = (((0,), (0,)), ((), ()))
 
 
 def half_mask(rows):
@@ -65,79 +66,107 @@
     )(chosen, key_rows, value_rows)
 
 
-def attend_kernel(
-    slot_ref, first_ref, q_ref, k_ref, v_ref, gk_ref, gv_ref, rand_ref, out_ref
-):
+def near_kernel(edge_ref, q_ref, k_ref, v_ref, gk_ref, gv_ref, acc_ref, stat_ref):
+    block = pl.program_id(0)
+    pairs = q_ref.shape[1] // (2 * HD)
+    low = half_mask(BLK)
+    rows = pl.ds(pl.multiple_of(block * BLK, BLK), 3 * BLK)
+    cut_low = jnp.where((block == 0) & (edge_ref[0] == 1), -1e30, 0.0)
+    cut_high = jnp.where((block == QB_DEV - 1) & (edge_ref[1] == 1), -1e30, 0.0)
+    zeros = jnp.zeros((BLK, 2 * HD), jnp.bfloat16)
+    lanes = lax.broadcasted_iota(jnp.int32, (HD, 2 * BLK), 1) < BLK
+    for pair in range(pairs):
+        cols = slice(pair * 2 * HD, (pair + 1) * 2 * HD)
+        query = q_ref[:, cols] * jnp.bfloat16(HD**-0.5)
+        stacked = jnp.concatenate(
+            [jnp.where(low, query, zeros), jnp.where(low, zeros, query)], axis=0
+        )
+        keys = jnp.concatenate([k_ref[rows, cols], gk_ref[:, cols]], axis=0)
+        values = jnp.concatenate([v_ref[rows, cols], gv_ref[:, cols]], axis=0)
+        near = lax.dot_general(keys, stacked, NT, preferred_element_type=jnp.float32)
+        near = jnp.concatenate(
+            [
+                near[:BLK] + cut_low,
+                near[BLK : 2 * BLK],
+                near[2 * BLK : 3 * BLK] + cut_high,
+                near[3 * BLK :],
+            ],
+            axis=0,
+        )
+        peak = jnp.max(near, axis=0, keepdims=True)
+        near = jnp.exp(near - peak)
+        stat_ref[0, pair, 0:1, :] = peak
+        stat_ref[0, pair, 1:2, :] = jnp.sum(near, axis=0, keepdims=True)
+        out = lax.dot_general(
+            values, near.astype(jnp.bfloat16), TT, preferred_element_type=jnp.float32
+        )
+        acc_ref[0, pair] = jnp.where(lanes, out[:HD], out[HD:])
+
+
+def far_kernel(slot_ref, q_ref, rand_ref, acc_ref, stat_ref, out_ref):
     block = pl.program_id(0)
     pairs = q_ref.shape[1] // (2 * HD)
     heads_here = 2 * pairs
     low = half_mask(BLK)
-    rows = pl.ds(pl.multiple_of(block * BLK, BLK), 3 * BLK)
-    cut_low = jnp.where((block == 0) & (first_ref[0] == 1), -1e30, 0.0)
-    cut_high = jnp.where((block == QB_DEV - 1) & (first_ref[1] == 1), -1e30, 0.0)
     zeros = jnp.zeros((BLK, 2 * HD), jnp.bfloat16)
+    lanes = lax.broadcasted_iota(jnp.int32, (HD, 2 * BLK), 1) < BLK
     for pair in range(pairs):
         cols = slice(pair * 2 * HD, (pair + 1) * 2 * HD)
         query = q_ref[:, cols] * jnp.bfloat16(HD**-0.5)
-        q_even = jnp.where(low, query, zeros)
-        q_odd = jnp.where(low, zeros, query)
-        stacked = jnp.concatenate([q_even, q_odd], axis=0)
         spread = jnp.concatenate(
             [
-                jnp.concatenate([q_even, zeros], axis=1),
-                jnp.concatenate([zeros, q_odd], axis=1),
+                jnp.concatenate([jnp.where(low, query, zeros), zeros], axis=1),
+                jnp.concatenate([zeros, jnp.where(low, zeros, query)], axis=1),
             ],
             axis=0,
         )
-        random_tiles = []
+        tiles = []
         for r in range(R):
             at = (block * heads_here + 2 * pair) * R + r
-            random_tiles.append(
+            tiles.append(
                 jnp.concatenate(
                     [rand_ref[slot_ref[at]], rand_ref[slot_ref[at + R]]], axis=1
                 )
             )
-        random_kv = jnp.concatenate(random_tiles, axis=0)
-        keys = jnp.concatenate([k_ref[rows, cols], gk_ref[:, cols]], axis=0)
-        values = jnp.concatenate([v_ref[rows, cols], gv_ref[:, cols]], axis=0)
-        near = lax.dot_general(keys, stacked, NT, preferred_element_type=jnp.float32)
+        random_kv = jnp.concatenate(tiles, axis=0)
         far = lax.dot_general(random_kv, spread, NT, preferred_element_type=jnp.float32)
-        near = jnp.concatenate(
-            [near[:BLK] + cut_low, near[BLK : 2 * BLK], near[2 * BLK : 3 * BLK] + cut_high, near[3 * BLK :]],
-            axis=0,
-        )
-        peak = jnp.maximum(
-            jnp.max(near, axis=0, keepdims=True), jnp.max(far, axis=0, keepdims=True)
-        )
-        near = jnp.exp(near - peak)
+        near_peak = stat_ref[0, pair, 0:1, :]
+        peak = jnp.maximum(near_peak, jnp.max(far, axis=0, keepdims=True))
+        factor = jnp.exp(near_peak - peak)
         far = jnp.exp(far - peak)
-        total = jnp.sum(near, axis=0, keepdims=True) + jnp.sum(far, axis=0, keepdims=True)
-        contract = (((0,), (0,)), ((), ()))
-        near_out = lax.dot_general(
-            values, near.astype(jnp.bfloat16), contract, preferred_element_type=jnp.float32
-        )
-        far_out = lax.dot_general(
-            random_kv, far.astype(jnp.bfloat16), contract, preferred_element_type=jnp.float32
-        )
-        even = near_out[:HD] + far_out[HD : 2 * HD]
-        odd = near_out[HD:] + far_out[2 * HD : 3 * HD]
-        lanes = lax.broadcasted_iota(jnp.int32, (HD, 2 * BLK), 1) < BLK
-        both = jnp.concatenate([jnp.where(lanes, even, 0.0), jnp.where(lanes, 0.0, odd)], axis=0)
-        both = (both / total).T
-        out_ref[:, cols] = (both[:BLK] + both[BLK:]).astype(jnp.bfloat16)
-
-
-def attend(slots, edges, query_rows, keys, values, global_k, global_v, received):
-    tokens, width = query_rows.shape
-
-    def whole(array):
-        return pl.BlockSpec(array.shape, lambda i, *_: (0,) * array.ndim)
-
+        total = stat_ref[0, pair, 1:2, :] * factor + jnp.sum(far, axis=0, keepdims=True)
+        out = lax.dot_general(
+            random_kv, far.astype(jnp.bfloat16), TT, preferred_element_type=jnp.float32
+        )
+        merged = acc_ref[0, pair] * factor + jnp.where(
+            lanes, out[HD : 2 * HD], out[2 * HD : 3 * HD]
+        )
+        merged = merged / total
+        split = jnp.concatenate(
+            [jnp.where(lanes, merged, 0.0), jnp.where(lanes, 0.0, merged)], axis=0
+        ).T
+        out_ref[:, cols] = (split[:BLK] + split[BLK:]).astype(jnp.bfloat16)
+
+
+def whole(array):
+    return pl.BlockSpec(array.shape, lambda i, *_: (0,) * array.ndim)
+
+
+def by_block(*shape):
+    return pl.BlockSpec((1,) + shape, lambda i, *_: (i,) + (0,) * len(shape))
+
+
+def attend_near(edges, query_rows, keys, values, global_k, global_v):
+    width = query_rows.shape[1]
+    pairs = width // (2 * HD)
     return pl.pallas_call(
-        attend_kernel,
-        out_shape=jax.ShapeDtypeStruct((tokens, width), jnp.bfloat16),
+        near_kernel,
+        out_shape=(
+            jax.ShapeDtypeStruct((QB_DEV, pairs, HD, 2 * BLK), jnp.float32),
+            jax.ShapeDtypeStruct((QB_DEV, pairs, 8, 2 * BLK), jnp.float32),
+        ),
         grid_spec=pltpu.PrefetchScalarGridSpec(
-            num_scalar_prefetch=2,
+            num_scalar_prefetch=1,
             grid=(QB_DEV,),
             in_specs=[
                 pl.BlockSpec((BLK, width), lambda i, *_: (i, 0)),
@@ -145,13 +174,46 @@
                 whole(values),
                 whole(global_k),
                 whole(global_v),
+            ],
+            out_specs=(by_block(pairs, HD, 2 * BLK), by_block(pairs, 8, 2 * BLK)),
+        ),
+        compiler_params=pltpu.CompilerParams(vmem_limit_bytes=VMEM_LIMIT),
+        cost_estimate=pl.CostEstimate(
+            flops=20_000_000_000, bytes_accessed=8_000_000, transcendentals=2_600_000
+        ),
+        name="attend_near",
+    )(edges, query_rows, keys, values, global_k, global_v)
+
+
+def attend_far(slots, query_rows, received, near_acc, near_stat):
+    tokens, width = query_rows.shape
+    pairs = width // (2 * HD)
+    return pl.pallas_call(
+        far_kernel,
+        out_shape=jax.ShapeDtypeStruct((tokens, width), jnp.bfloat16),
+        grid_spec=pltpu.PrefetchScalarGridSpec(
+            num_scalar_prefetch=1,
+            grid=(QB_DEV,),
+            in_specs=[
+                pl.BlockSpec((BLK, width), lambda i, *_: (i, 0)),
                 whole(received),
+                by_block(pairs, HD, 2 * BLK),
+                by_block(pairs, 8, 2 * BLK),
             ],
             out_specs=pl.BlockSpec((BLK, width), lambda i, *_: (i, 0)),
         ),
         compiler_params=pltpu.CompilerParams(vmem_limit_bytes=VMEM_LIMIT),
-        name="attend",
-    )(slots, edges, query_rows, keys, values, global_k, global_v, received)
+        cost_estimate=pl.CostEstimate(
+            flops=15_000_000_000, bytes_accessed=10_000_000, transcendentals=1_600_000
+        ),
+        name="attend_far",
+    )(slots, query_rows, received, near_acc, near_stat)
+
+
+def merge_parts(peak, total, accum):
+    top = jnp.max(peak, axis=0)
+    factor = jnp.exp(peak - top)
+    return top, jnp.sum(total * factor, axis=0), jnp.sum(accum * factor[..., None], axis=0)
 
 
 def local(
@@ -202,24 +264,14 @@
     my_rank = jnp.sum(jnp.where(by_owner, ranks[GROUP:], 0), axis=0)
     slots = owner * capacity + my_rank
 
-    sections = pack(chosen.reshape(slot_count), key_rows, value_rows)
     groups = [
         list(range(start, start + GROUP)) for start in range(0, shard_count, GROUP)
     ]
-    received = lax.all_to_all(
-        sections, "seq", 0, 0, axis_index_groups=groups, tiled=True
-    )
-
-    other_out = lax.ppermute(out_weight, "mp", swap)
-    other_up = lax.ppermute(up_weight, "mp", swap)
-    other_down = lax.ppermute(down_weight, "mp", swap)
-
     both = jnp.stack([key_rows, value_rows], axis=0)
     forward = [(i, i + 1) for i in range(shard_count - 1)]
     backward = [(i + 1, i) for i in range(shard_count - 1)]
     below = lax.ppermute(both[:, tok_rows - BLK :], "seq", forward)
     above = lax.ppermute(both[:, :BLK], "seq", backward)
-    padded = jnp.concatenate([below, both, above], axis=1)
 
     packed = jnp.stack([query_rows, key_rows, value_rows], axis=0)
     contributions = []
@@ -238,7 +290,7 @@
         jnp.einsum("qhd,thd->hqt", global_q, key_heads, preferred_element_type=jnp.float32)
         * score_scale
     )
-    seg_peak = jnp.max(global_scores, axis=2)
+    seg_peak = lax.reduce_precision(jnp.max(global_scores, axis=2), 8, 7)
     seg_weights = jnp.exp(global_scores - seg_peak[..., None])
     seg_total = jnp.sum(seg_weights, axis=2)
     seg_acc = jnp.einsum(
@@ -247,19 +299,64 @@
         value_heads,
         preferred_element_type=jnp.float32,
     )
-    stats = lax.all_gather(jnp.stack([seg_peak, seg_total], axis=0), "seq")
-    top = jnp.max(stats[:, 0], axis=0)
-    merged_total = jnp.sum(jnp.exp(stats[:, 0] - top) * stats[:, 1], axis=0)
-    factor = jnp.exp(seg_peak - top) / merged_total
-    global_out = lax.psum(seg_acc * factor[..., None], "seq")
+    total_high = lax.reduce_precision(seg_total, 8, 7)
+    total_low = seg_total - total_high
+    merge_rows = heads_here * GLOB * BLK // GROUP
+    stats = jnp.stack([seg_peak, total_high, total_low], axis=-1)
+    part = jnp.concatenate(
+        [
+            seg_acc,
+            stats,
+            jnp.zeros(seg_acc.shape[:2] + (HD - stats.shape[-1],), jnp.float32),
+        ],
+        axis=-1,
+    ).astype(jnp.bfloat16)
+    part = part.reshape(GROUP, 1, merge_rows, 2 * HD)
+
+    tiles = pack(chosen.reshape(slot_count), key_rows, value_rows)
+    tiles = tiles.reshape(GROUP, capacity, BLK, 2 * HD)
+    tiles, part, below, above = lax.optimization_barrier((tiles, part, below, above))
+    received, parts = (
+        lax.all_to_all(block, "seq", 0, 0, axis_index_groups=groups, tiled=True)
+        for block in (tiles, part)
+    )
+    received = received.reshape(slot_count, BLK, 2 * HD)
+
+    other_out = lax.ppermute(out_weight, "mp", swap)
+    other_up = lax.ppermute(up_weight, "mp", swap)
+    other_down = lax.ppermute(down_weight, "mp", swap)
+
+    edges = jnp.stack([my_shard == 0, my_shard == shard_count - 1]).astype(jnp.int32)
+    padded = jnp.concatenate([below, both, above], axis=1)
+    near_acc, near_stat = attend_near(
+        edges, query_rows, padded[0], padded[1], global_k, global_v
+    )
+
+    parts = parts[:, 0].astype(jnp.float32)
+    merged = merge_parts(
+        parts[..., HD], parts[..., HD + 1] + parts[..., HD + 2], parts[..., :HD]
+    )
+    if shard_count > GROUP:
+        across = [list(range(at, shard_count, GROUP)) for at in range(GROUP)]
+        merged = merge_parts(
+            *(lax.all_gather(one, "seq", axis_index_groups=across) for one in merged)
+        )
+    merged_rows = (merged[2] / merged[1][:, None]).astype(jnp.bfloat16)
+    global_rows = lax.all_to_all(
+        jnp.broadcast_to(merged_rows[None], (GROUP,) + merged_rows.shape),
+        "seq",
+        0,
+        0,
+        axis_index_groups=groups,
+        tiled=True,
+    )
     global_rows = (
-        global_out.transpose(1, 0, 2).reshape(GLOB * BLK, local_width).astype(jnp.bfloat16)
-    )
-
-    edges = jnp.stack([my_shard == 0, my_shard == shard_count - 1]).astype(jnp.int32)
-    attention = attend(
-        slots, edges, query_rows, padded[0], padded[1], global_k, global_v, received
-    )
+        global_rows.reshape(heads_here, GLOB * BLK, HD)
+        .transpose(1, 0, 2)
+        .reshape(GLOB * BLK, local_width)
+    )
+
+    attention = attend_far(slots, query_rows, received, near_acc, near_stat)
     for which in range(GLOB):
         global_id = global_blocks[which]
         start_row = global_id % QB_DEV * BLK

time: 420 us -> 352 us (0.84)
  the two profiles are of different devices: /device:TPU:0 before, /device:TPU:17 now
where the time goes in v2:
time: 352 us; the launch traced here: 350 us
  waiting for transfers between devices  200 us (57%)
  Pallas kernels  38.1 us (11%)
  matrix products  24.2 us (7%)
  starting transfers between devices  24 us (7%)
  blocking collectives  21.3 us (6%)
  between operations  19.2 us (5%)
  local copies, waits for them, and re-layouts  11.6 us (3%)
  other arithmetic  11.6 us (3%)
    all_to_all x1, waiting for transfers between devices, local(): lax.all_to_all(block, 'seq', 0, 0, axis_index_groups=groups, tiled=True)  110 us
    psum x1, waiting for transfers between devices, local(): global_qkv = lax.psum(jnp.concatenate(contributions, axis=1), 'seq')  88.4 us
    dot_general x2, matrix products, local(): total = total + jnp.dot(hidden, down, preferred_element_type=jnp.float32)  18.2 us
    pallas_call x1, Pallas kernels, attend_far(): pl.pallas_call(far_kernel, out_shape=jax.ShapeDtypeStruct((tokens, width)...  17.3 us
    pallas_call x1, Pallas kernels, attend_near(): pl.pallas_call(near_kernel, out_shape=(jax.ShapeDtypeStruct((QB_DEV, pair...  14.5 us
    all_to_all x1, blocking collectives, local(): lax.all_to_all(block, 'seq', 0, 0, axis_index_groups=groups, tiled=True)  11.8 us
    all_to_all x1, blocking collectives, local(): lax.all_to_all(jnp.broadcast_to(merged_rows[None], (GROUP,) + merged_rows...  9.51 us
  transfers between devices with their start and end apart: 9, of which 3 were waited for; matrix products, arithmetic and copies ran while one was open for 9% of the time, Pallas kernels for 11%

profile of v2, /device:TPU:17, one launch (start us, length us, event | category | flops | bytes accessed | tf_op | source)
XLA Modules:
  0.0 350.4 jit_solution(8944018967561764352)
XLA Ops:
  6.5 1.5 fusion.101
  13.4 2.2 pad_maximum_fusion
  15.7 0.8 pad_maximum_fusion.3
  16.6 0.7 pad_maximum_fusion.4
  17.3 3.1 collective-permute-start
  20.4 4.0 %collective-permute-start.1 = (bf16[2,64,512]{2,1,0:T(8,128)(2,1)}, bf16[2,64,512]{2,1,0:T(8,128)(2,1)S(1)}, u32[]{:S(2)}, u32[]{:S(2)}) collective-permute-start(bf16[2,64,512]{2,1,0:T(8,128)(2,1)} %get-tuple-element.23), channel_id=1, source_target_pairs={{2,0},{4,2},{6,4},{8,6},{10,8},{12,10},{14,12},{16,14},{18,16},{20... | collective-permute-start | bytes 393224 | tf_op jit(solution)/shard_map/ppermute | solution.py:274
  24.4 0.4 copy.35
  24.8 0.5 reshape.251
  25.4 0.2 convolution_convert_fusion
  25.6 0.5 copy.38
  26.1 0.5 copy.37
  26.7 0.4 select_reduce_fusion
  27.1 0.7 reshape.252.index_ref
  27.7 6.3 %pack.1 = bf16[384,64,128]{2,1,0:T(8,128)(2,1)} custom-call(s32[384]{0:T(512)} %reshape.252.index_ref, bf16[1024,512]{1,0:T(8,128)(2,1)} %key_ref.1, bf16[1024,512]{1,0:T(8,128)(2,1)} %value_ref.1), custom_call_target="tpu_custom_call" | custom-call | tf_op jit(solution)/shard_map/pack/pallas_call | solution.py:54
  34.1 88.4 %all-reduce.2.cloned.1.call-done = bf16[3,128,512]{2,1,0:T(8,128)(2,1)} async-done(((bf16[3,128,512]{2,1,0:T(8,128)(2,1)}), bf16[3,128,512]{2,1,0:T(8,128)(2,1)}) %all-reduce.2.cloned.1.call-update) | async-done | bytes 393232 | tf_op jit(solution)/shard_map/psum | solution.py:283
  122.5 1.7 slice_bitcast_fusion.2
  124.4 0.8 multiply_reduce_fusion
  125.2 0.9 fusion.16
  126.1 1.0 fusion.43
  127.6 0.5 copy.40
  128.1 11.8 %all_to_all.15 = bf16[16,1,64,128]{3,2,1,0:T(8,128)(2,1)S(1)} all-to-all(bf16[16,1,64,128]{3,2,1,0:T(8,128)(2,1)S(1)} %copy.40), channel_id=1, replica_groups={{0,2,4,6,8,10,12,14,16,18,20,22,24,26,28,30},{1,3,5,7,9,11,13,15,17,19,..., dimensions={0} | all-to-all | bytes 524288 | tf_op jit(solution)/shard_map/all_to_all | solution.py:320
  139.8 0.4 copy.41
  140.6 0.2 reshape.261
  140.9 9.5 %all_to_all.16 = bf16[16,2,2048]{2,1,0:T(2,128)(2,1)S(1)} all-to-all(bf16[16,2,2048]{2,1,0:T(2,128)(2,1)S(1)} %reshape.261), channel_id=1, replica_groups={{0,2,4,6,8,10,12,14,16,18,20,22,24,26,28,30},{1,3,5,7,9,11,13,15,17,19,..., dimensions={0} | all-to-all | bytes 262144 | tf_op jit(solution)/shard_map/all_to_all | solution.py:345
  150.4 6.4 %all-to-all-start = ((bf16[16,24,64,128]{3,2,1,0:T(8,128)(2,1)}), bf16[16,24,64,128]{3,2,1,0:T(8,128)(2,1)}, u32[]{:S(2)}, u32[]{:S(2)}) async-start(bf16[16,24,64,128]{3,2,1,0:T(8,128)(2,1)} %bitcast.69), calls=%async_computation | async-start | bytes 12582912 | tf_op jit(solution)/shard_map/all_to_all | solution.py:320
  156.8 5.4 %collective-permute-start.3 = (bf16[512,1024]{1,0:T(8,128)(2,1)S(1)}, bf16[512,1024]{1,0:T(8,128)(2,1)}, u32[]{:S(2)}, u32[]{:S(2)}) collective-permute-start(bf16[512,1024]{1,0:T(8,128)(2,1)S(1)} %copy-done.4), channel_id=1, source_target_pairs={{0,1},{1,0},{2,3},{3,2},{4,5},{5,4},{6,7},{7,6},{8,9},{9,8},{10,11... | collective-permute-start | bytes 3145736 | tf_op jit(solution)/shard_map/ppermute | solution.py:325
  162.3 0.4 collective-permute-start.4
  162.8 0.7 add_convert_fusion.1.edge_ref
  163.4 0.6 fusion.70.slot_ref
  164.2 1.6 slice_bitcast_fusion
  165.8 14.5 %attend_near.1 = (f32[16,4,64,128]{3,2,1,0:T(8,128)}, f32[16,4,8,128]{3,2,1,0:T(8,128)}) custom-call(s32[2]{0:T(128)} %add_convert_fusion.1.edge_ref, bf16[1024,512]{1,0:T(8,128)(2,1)} %q_ref.3, bf16[1152,512]{1,0:T(8,128)(2,1)} %get-tuple-element.22.k_ref, bf16[1152,512]{1,0:T(8,128)(2,1)} %get-tuple-element.21.v_ref, ...), custom_call_target="tpu_custom_call" | custom-call | flops 20000000000 | bytes 8000000 | tf_op jit(solution)/shard_map/attend_near/pallas_call | solution.py:162
  180.3 0.2 reshape.262
  180.5 0.2 copy.42
  181.3 0.2 copy.44
  181.6 110.1 %all-to-all-done = bf16[16,24,64,128]{3,2,1,0:T(8,128)(2,1)} async-done(((bf16[16,24,64,128]{3,2,1,0:T(8,128)(2,1)}), bf16[16,24,64,128]{3,2,1,0:T(8,128)(2,1)}, u32[]{:S(2)}, u32[]{:S(2)}) %all-to-all-start) | async-done | bytes 6291488 | tf_op jit(solution)/shard_map/all_to_all | solution.py:320
  291.6 17.3 %attend_far.1 = bf16[1024,512]{1,0:T(8,128)(2,1)} custom-call(s32[384]{0:T(512)} %fusion.70.slot_ref, bf16[1024,512]{1,0:T(8,128)(2,1)} %q_ref.3, bf16[384,64,128]{2,1,0:T(8,128)(2,1)} %bitcast.11.rand_ref, f32[16,4,64,128]{3,2,1,0:T(8,128)} %get-tuple-element.14.acc_ref, f32[16,4,8,128]{3,2,1,0:T(8,128)} %get-tuple-element.15.stat_ref), custom_call_target="tpu_custom_call" | custom-call | flops 15000000512 | bytes 10000000 | tf_op jit(solution)/shard_map/attend_far/pallas_call | solution.py:191
  308.9 1.5 select_dynamic-update-slice_fusion.1
  310.4 1.5 select_dynamic-update-slice_fusion
  311.9 1.1 constant_dynamic-slice_fusion.1
  313.0 4.5 %collective-permute-start.2 = (bf16[512,512]{1,0:T(8,128)(2,1)S(1)}, bf16[512,512]{1,0:T(8,128)(2,1)S(1)}, u32[]{:S(2)}, u32[]{:S(2)}) collective-permute-start(bf16[512,512]{1,0:T(8,128)(2,1)S(1)} %constant_dynamic-slice_fusion.1), channel_id=1, source_target_pairs={{0,1},{1,0},{2,3},{3,2},{4,5},{5,4},{6,7},{7,6},{8,9},{9,8},{10,11... | collective-permute-start | bytes 1572872 | tf_op jit(solution)/shard_map/ppermute | solution.py:373
  317.4 1.9 fusion.48
  319.4 2.1 convert_reduce_fusion
  321.5 0.4 fusion.20
  321.9 9.5 %fusion.29 = f32[512,1024]{1,0:T(8,128)} fusion(bf16[2048,1024]{1,0:T(8,128)(2,1)} %param.19, bf16[1024,2048]{1,0:T(8,128)(2,1)} %param.18, bf16[512,1024]{1,0:T(8,128)(2,1)S(1)} %get-tuple-element.41, f32[1024]{0:T(1024)S(1)} %copy-done.7, f32[512]{0:T(512)S(1)} %add_rsqrt_fusion, f32[512]{0:T(512)S(1)} %broadcast_multiply_fusion), kind=kOutput, calls=%fused_computation.36 | convolution fusion | flops 4307025920 | bytes 11542528 | tf_op jit(solution)/shard_map/dot_general | solution.py:391
  331.4 8.7 %fusion.24 = bf16[512,1024]{1,0:T(8,128)(2,1)S(1)} fusion(f32[512,1024]{1,0:T(8,128)} %fusion.29, bf16[512,1024]{1,0:T(8,128)(2,1)S(1)} %get-tuple-element.41, bf16[2048,1024]{1,0:T(8,128)(2,1)} %collective-permute-done.5, bf16[1024,2048]{1,0:T(8,128)(2,1)} %collective-permute-done.4, f32[1024]{0:T(1024)S(1)} %copy-done.7, f32[512]{0:T(512)S(1)} %add_rsqrt_fusion, ...), kind=kOutput, calls=%fused_computation.33 | convolution fusion | flops 4309123072 | bytes 12591104 | tf_op jit(solution)/shard_map/dot_general | solution.py:391
  340.3 1.9 collective-permute-done.6
  342.2 0.3 broadcast_select_fusion.1
  342.5 1.0 pad_maximum_fusion.2
  (59 shorter events, 2.2 us)
Async XLA Ops:
  6.5 10.0 %copy-start.2 = (bf16[1024,512]{1,0:T(8,128)(2,1)S(1)}, bf16[1024,512]{1,0:T(8,128)(2,1)}, u32[]{:S(2)}) copy-start(bf16[1024,512]{1,0:T(8,128)(2,1)} %value_ref.1) | copy-start | bytes 3145732
  6.5 10.0 %copy-start = (bf16[1024,512]{1,0:T(8,128)(2,1)S(1)}, bf16[1024,512]{1,0:T(8,128)(2,1)}, u32[]{:S(2)}) copy-start(bf16[1024,512]{1,0:T(8,128)(2,1)} %key_ref.1) | copy-start | bytes 3145732
  6.5 116.0 %all-reduce.2.cloned.1.call-start = ((), (), s32[]{:S(2)}) async-start(), calls=%async_computation.3 | async-start | bytes 786432 | tf_op jit(solution)/shard_map/psum | solution.py:283
  13.4 10.9 %copy-start.6 = (s32[256,8,3]{0,1,2:T(8,128)S(1)}, s32[256,8,3]{0,1,2:T(8,128)}, u32[]{:S(2)}) copy-start(s32[256,8,3]{0,1,2:T(8,128)} %param.14) | copy-start | bytes 73732
  17.3 110.3 %collective-permute-start = (bf16[2,64,512]{2,1,0:T(8,128)(2,1)}, bf16[2,64,512]{2,1,0:T(8,128)(2,1)S(1)}, u32[]{:S(2)}, u32[]{:S(2)}) collective-permute-start(bf16[2,64,512]{2,1,0:T(8,128)(2,1)} %get-tuple-element.24), channel_id=1, source_target_pairs={{0,2},{2,4},{4,6},{6,8},{8,10},{10,12},{12,14},{14,16},{16,18},{18... | collective-permute-start | bytes 393224 | tf_op jit(solution)/shard_map/ppermute | solution.py:273
  20.4 107.2 %collective-permute-start.1 = (bf16[2,64,512]{2,1,0:T(8,128)(2,1)}, bf16[2,64,512]{2,1,0:T(8,128)(2,1)S(1)}, u32[]{:S(2)}, u32[]{:S(2)}) collective-permute-start(bf16[2,64,512]{2,1,0:T(8,128)(2,1)} %get-tuple-element.23), channel_id=1, source_target_pairs={{2,0},{4,2},{6,4},{8,6},{10,8},{12,10},{14,12},{16,14},{18,16},{20... | collective-permute-start | bytes 393224 | tf_op jit(solution)/shard_map/ppermute | solution.py:274
  150.4 6.4 %copy-start.4 = (bf16[512,1024]{1,0:T(8,128)(2,1)S(1)}, bf16[512,1024]{1,0:T(8,128)(2,1)}, u32[]{:S(2)}) copy-start(bf16[512,1024]{1,0:T(8,128)(2,1)} %param.16) | copy-start | bytes 3145732
  150.4 13.7 %copy-start.1 = (bf16[1024,512]{1,0:T(8,128)(2,1)S(1)}, bf16[1024,512]{1,0:T(8,128)(2,1)}, u32[]{:S(2)}) copy-start(bf16[1024,512]{1,0:T(8,128)(2,1)} %key_ref.1) | copy-start | bytes 3145732
  150.4 13.7 %copy-start.3 = (bf16[1024,512]{1,0:T(8,128)(2,1)S(1)}, bf16[1024,512]{1,0:T(8,128)(2,1)}, u32[]{:S(2)}) copy-start(bf16[1024,512]{1,0:T(8,128)(2,1)} %value_ref.1) | copy-start | bytes 3145732
  150.4 141.3 %all-to-all-start = ((bf16[16,24,64,128]{3,2,1,0:T(8,128)(2,1)}), bf16[16,24,64,128]{3,2,1,0:T(8,128)(2,1)}, u32[]{:S(2)}, u32[]{:S(2)}) async-start(bf16[16,24,64,128]{3,2,1,0:T(8,128)(2,1)} %bitcast.69), calls=%async_computation | async-start | bytes 12582912 | tf_op jit(solution)/shard_map/all_to_all | solution.py:320
  156.8 162.5 %collective-permute-start.3 = (bf16[512,1024]{1,0:T(8,128)(2,1)S(1)}, bf16[512,1024]{1,0:T(8,128)(2,1)}, u32[]{:S(2)}, u32[]{:S(2)}) collective-permute-start(bf16[512,1024]{1,0:T(8,128)(2,1)S(1)} %copy-done.4), channel_id=1, source_target_pairs={{0,1},{1,0},{2,3},{3,2},{4,5},{5,4},{6,7},{7,6},{8,9},{9,8},{10,11... | collective-permute-start | bytes 3145736 | tf_op jit(solution)/shard_map/ppermute | solution.py:325
  162.2 169.2 %collective-permute-start.5 = (bf16[2048,1024]{1,0:T(8,128)(2,1)}, bf16[2048,1024]{1,0:T(8,128)(2,1)}, u32[]{:S(2)}, u32[]{:S(2)}) collective-permute-start(bf16[2048,1024]{1,0:T(8,128)(2,1)} %param.19), channel_id=1, source_target_pairs={{0,1},{1,0},{2,3},{3,2},{4,5},{5,4},{6,7},{7,6},{8,9},{9,8},{10,11... | collective-permute-start | bytes 12582920 | tf_op jit(solution)/shard_map/ppermute | solution.py:327
  162.3 169.1 %collective-permute-start.4 = (bf16[1024,2048]{1,0:T(8,128)(2,1)}, bf16[1024,2048]{1,0:T(8,128)(2,1)}, u32[]{:S(2)}, u32[]{:S(2)}) collective-permute-start(bf16[1024,2048]{1,0:T(8,128)(2,1)} %param.18), channel_id=1, source_target_pairs={{0,1},{1,0},{2,3},{3,2},{4,5},{5,4},{6,7},{7,6},{8,9},{9,8},{10,11... | collective-permute-start | bytes 12582920 | tf_op jit(solution)/shard_map/ppermute | solution.py:326
  313.0 6.4 %collective-permute-start.2 = (bf16[512,512]{1,0:T(8,128)(2,1)S(1)}, bf16[512,512]{1,0:T(8,128)(2,1)S(1)}, u32[]{:S(2)}, u32[]{:S(2)}) collective-permute-start(bf16[512,512]{1,0:T(8,128)(2,1)S(1)} %constant_dynamic-slice_fusion.1), channel_id=1, source_target_pairs={{0,1},{1,0},{2,3},{3,2},{4,5},{5,4},{6,7},{7,6},{8,9},{9,8},{10,11... | collective-permute-start | bytes 1572872 | tf_op jit(solution)/shard_map/ppermute | solution.py:373
  317.4 1.9 copy-start.5
  319.3 2.6 copy-start.7
  340.2 2.0 collective-permute-start.6
Sparse Core Ops, SparseCore 0:
  16.7 105.7 all-reduce.1

commit v3 on v2

--- a/solution.py
+++ b/solution.py
@@ -280,7 +280,13 @@
         block_rows = lax.dynamic_slice_in_dim(packed, global_id % QB_DEV * BLK, BLK, 1)
         is_owner = global_id // QB_DEV == my_shard
         contributions.append(jnp.where(is_owner, block_rows, jnp.zeros_like(block_rows)))
-    global_qkv = lax.psum(jnp.concatenate(contributions, axis=1), "seq")
+    contributed = jnp.concatenate(contributions, axis=1)
+    shares = contributed.reshape(shard_count, -1, local_width)
+    shares = lax.all_to_all(shares, "seq", 0, 0, tiled=True)
+    share = jnp.sum(shares.astype(jnp.float32), axis=0).astype(jnp.bfloat16)
+    global_qkv = lax.all_to_all(
+        jnp.broadcast_to(share[None], (shard_count,) + share.shape), "seq", 0, 0, tiled=True
+    ).reshape(contributed.shape)
     global_q = global_qkv[0].reshape(GLOB * BLK, heads_here, HD)
     global_k, global_v = global_qkv[1], global_qkv[2]
 
@@ -315,7 +321,6 @@
 
     tiles = pack(chosen.reshape(slot_count), key_rows, value_rows)
     tiles = tiles.reshape(GROUP, capacity, BLK, 2 * HD)
-    tiles, part, below, above = lax.optimization_barrier((tiles, part, below, above))
     received, parts = (
         lax.all_to_all(block, "seq", 0, 0, axis_index_groups=groups, tiled=True)
         for block in (tiles, part)

time: 352 us -> 292 us (0.83)
  waiting for transfers between devices: 200 us -> 143 us
  between operations: 19.2 us -> 5.57 us
  starting transfers between devices: 24 us -> 35.7 us
  blocking collectives: 21.3 us -> 16.8 us
    ppermute x1, waiting for transfers between devices: 0.01 us -> 126 us  [local(): above = lax.ppermute(both[:, :BLK], 'seq', backward)]
    all_to_all x1 -> x2, waiting for transfers between devices: 110 us -> 6.88 us  [local(): lax.all_to_all(block, 'seq', 0, 0, axis_index_groups=groups, tiled=True)]
    psum x1 -> x0, waiting for transfers between devices: 88.4 us -> none  [local(): global_qkv = lax.psum(jnp.concatenate(contributions, axis=1), 'seq')]
    all_to_all x0 -> x2, starting transfers between devices: none -> 10.6 us  [the longest x1 5.36 us: local(): lax.all_to_all(jnp.broadcast_to(merged_rows[None], (GROUP,) + merged_rows...]
    all_to_all x0 -> x2, waiting for transfers between devices: none -> 5.97 us  [the longest x1 5.96 us: local(): lax.all_to_all(jnp.broadcast_to(share[None], (shard_count,) + share.shape...]
    all_to_all x1 -> x2, starting transfers between devices: 6.44 us -> 11.8 us  [local(): lax.all_to_all(block, 'seq', 0, 0, axis_index_groups=groups, tiled=True)]
    all_to_all x2 -> x1, blocking collectives: 21.3 us -> 16.8 us  [local(): shares = lax.all_to_all(shares, 'seq', 0, 0, tiled=True)]
  transfers between devices with their start and end apart: 9 -> 11, of which waited for: 3 -> 5; matrix products, arithmetic and copies ran while one was open for 9% -> 10% of each run, Pallas kernels for 11% -> 13%
where the time goes in v3:
time: 292 us; the launch traced here: 290 us
  waiting for transfers between devices  143 us (49%)
  Pallas kernels  38.3 us (13%)
  starting transfers between devices  35.7 us (12%)
  matrix products  24.2 us (8%)
  blocking collectives  16.8 us (6%)
  local copies, waits for them, and re-layouts  13.9 us (5%)
  other arithmetic  12.4 us (4%)
  between operations  5.57 us (2%)
    ppermute x1, waiting for transfers between devices, local(): above = lax.ppermute(both[:, :BLK], 'seq', backward)  126 us
    dot_general x2, matrix products, local(): total = total + jnp.dot(hidden, down, preferred_element_type=jnp.float32)  18.2 us
    pallas_call x1, Pallas kernels, attend_far(): pl.pallas_call(far_kernel, out_shape=jax.ShapeDtypeStruct((tokens, width)...  17.3 us
    all_to_all x1, blocking collectives, local(): shares = lax.all_to_all(shares, 'seq', 0, 0, tiled=True)  16.8 us
    pallas_call x1, Pallas kernels, attend_near(): pl.pallas_call(near_kernel, out_shape=(jax.ShapeDtypeStruct((QB_DEV, pair...  14.7 us
    all_to_all x2, starting transfers between devices, local(): lax.all_to_all(block, 'seq', 0, 0, axis_index_groups=groups, tiled=True)  11.8 us
    all_to_all x2, waiting for transfers between devices, local(): lax.all_to_all(block, 'seq', 0, 0, axis_index_groups=groups, tiled=True)  6.88 us
    pallas_call x1, Pallas kernels, pack(): pl.pallas_call(pack_kernel, out_shape=jax.ShapeDtypeStruct((slots, BLK, 2...  6.32 us
  transfers between devices with their start and end apart: 11, of which 5 were waited for; matrix products, arithmetic and copies ran while one was open for 10% of the time, Pallas kernels for 13%

profile of v3, /device:TPU:17, one launch (start us, length us, event | category | flops | bytes accessed | tf_op | source)
XLA Modules:
  0.0 290.3 jit_solution(5930499858298372534)
XLA Ops:
  0.0 1.3 fusion.102
  6.5 2.3 pad_maximum_fusion
  9.0 16.8 %all_to_all.25 = bf16[16,24,512]{2,1,0:T(8,128)(2,1)S(1)} all-to-all(bf16[16,24,512]{2,1,0:T(8,128)(2,1)S(1)} %bitcast.75), channel_id=1, replica_groups=mesh['seq'=16,'mp'=2] {'seq'}, dimensions={0} | all-to-all | bytes 786432 | tf_op jit(solution)/shard_map/all_to_all | solution.py:285
  25.9 0.8 broadcast_in_dim.22
  26.6 5.3 %all-to-all-start.2 = ((bf16[16,24,512]{2,1,0:T(8,128)(2,1)}), bf16[16,24,512]{2,1,0:T(8,128)(2,1)S(1)}, u32[]{:S(2)}, u32[]{:S(2)}) async-start(bf16[16,24,512]{2,1,0:T(8,128)(2,1)} %broadcast_in_dim.22), calls=%async_computation.2 | async-start | bytes 786432 | tf_op jit(solution)/shard_map/all_to_all | solution.py:287
  31.9 0.5 copy.38
  32.5 0.5 copy.37
  33.0 1.2 copy.35
  34.2 1.1 reshape.258
  35.3 0.7 fusion.76
  36.0 6.0 %all-to-all-done.2 = bf16[16,24,512]{2,1,0:T(8,128)(2,1)S(1)} async-done(((bf16[16,24,512]{2,1,0:T(8,128)(2,1)}), bf16[16,24,512]{2,1,0:T(8,128)(2,1)S(1)}, u32[]{:S(2)}, u32[]{:S(2)}) %all-to-all-start.2) | async-done | bytes 393248 | tf_op jit(solution)/shard_map/all_to_all | solution.py:287
  42.0 0.7 fusion.99
  42.8 0.8 multiply_reduce_fusion
  43.7 0.9 fusion.16
  44.6 1.0 fusion.43
  46.1 1.1 copy.40
  47.3 5.1 %all-to-all-start.3 = ((bf16[16,1,64,128]{3,2,1,0:T(8,128)(2,1)}), bf16[16,1,64,128]{3,2,1,0:T(8,128)(2,1)S(1)}, u32[]{:S(2)}, u32[]{:S(2)}) async-start(bf16[16,1,64,128]{3,2,1,0:T(8,128)(2,1)} %copy.40), calls=%async_computation.3 | async-start | bytes 524288 | tf_op jit(solution)/shard_map/all_to_all | solution.py:325
  52.7 6.9 %all-to-all-done.3 = bf16[16,1,64,128]{3,2,1,0:T(8,128)(2,1)S(1)} async-done(((bf16[16,1,64,128]{3,2,1,0:T(8,128)(2,1)}), bf16[16,1,64,128]{3,2,1,0:T(8,128)(2,1)S(1)}, u32[]{:S(2)}, u32[]{:S(2)}) %all-to-all-start.3) | async-done | bytes 262176 | tf_op jit(solution)/shard_map/all_to_all | solution.py:325
  59.5 0.4 copy.41
  60.3 0.9 reshape.270
  61.2 5.4 %all-to-all-start.4 = ((bf16[16,2,2048]{2,1,0:T(2,128)(2,1)}), bf16[16,2,2048]{2,1,0:T(2,128)(2,1)S(1)}, u32[]{:S(2)}, u32[]{:S(2)}) async-start(bf16[16,2,2048]{2,1,0:T(2,128)(2,1)} %reshape.270), calls=%async_computation.4 | async-start | bytes 262144 | tf_op jit(solution)/shard_map/all_to_all | solution.py:350
  66.9 0.7 reshape.259.index_ref
  67.6 6.3 %pack.1 = bf16[384,64,128]{2,1,0:T(8,128)(2,1)} custom-call(s32[384]{0:T(512)} %reshape.259.index_ref, bf16[1024,512]{1,0:T(8,128)(2,1)} %key_ref.1, bf16[1024,512]{1,0:T(8,128)(2,1)} %value_ref.1), custom_call_target="tpu_custom_call" | custom-call | tf_op jit(solution)/shard_map/pack/pallas_call | solution.py:54
  74.0 6.6 %all-to-all-start = ((bf16[16,24,64,128]{3,2,1,0:T(8,128)(2,1)}), bf16[16,24,64,128]{3,2,1,0:T(8,128)(2,1)}, u32[]{:S(2)}, u32[]{:S(2)}) async-start(bf16[16,24,64,128]{3,2,1,0:T(8,128)(2,1)} %bitcast.71), calls=%async_computation | async-start | bytes 12582912 | tf_op jit(solution)/shard_map/all_to_all | solution.py:325
  80.6 0.7 pad_maximum_fusion.5
  81.3 4.0 %collective-permute-start.1 = (bf16[2,64,512]{2,1,0:T(8,128)(2,1)}, bf16[2,64,512]{2,1,0:T(8,128)(2,1)S(1)}, u32[]{:S(2)}, u32[]{:S(2)}) collective-permute-start(bf16[2,64,512]{2,1,0:T(8,128)(2,1)} %get-tuple-element.16), channel_id=1, source_target_pairs={{2,0},{4,2},{6,4},{8,6},{10,8},{12,10},{14,12},{16,14},{18,16},{20... | collective-permute-start | bytes 393224 | tf_op jit(solution)/shard_map/ppermute | solution.py:274
  85.3 1.9 collective-permute-start
  87.2 3.1 %collective-permute-start.3 = (bf16[512,1024]{1,0:T(8,128)(2,1)S(1)}, bf16[512,1024]{1,0:T(8,128)(2,1)}, u32[]{:S(2)}, u32[]{:S(2)}) collective-permute-start(bf16[512,1024]{1,0:T(8,128)(2,1)S(1)} %copy-done.4), channel_id=1, source_target_pairs={{0,1},{1,0},{2,3},{3,2},{4,5},{5,4},{6,7},{7,6},{8,9},{9,8},{10,11... | collective-permute-start | bytes 3145736 | tf_op jit(solution)/shard_map/ppermute | solution.py:330
  90.3 0.4 collective-permute-start.4
  90.8 0.5 fusion.70.slot_ref
  91.3 0.6 add_convert_fusion.1.edge_ref
  91.9 126.1 %collective-permute-done.1 = bf16[2,64,512]{2,1,0:T(8,128)(2,1)S(1)} collective-permute-done((bf16[2,64,512]{2,1,0:T(8,128)(2,1)}, bf16[2,64,512]{2,1,0:T(8,128)(2,1)S(1)}, u32[]{:S(2)}, u32[]{:S(2)}) %collective-permute-start.1) | collective-permute-done | bytes 131104 | tf_op jit(solution)/shard_map/ppermute | solution.py:274
  218.1 2.5 collective-permute-done
  220.6 1.1 pad_maximum_fusion.1
  221.6 1.6 slice_bitcast_fusion
  223.2 14.7 %attend_near.1 = (f32[16,4,64,128]{3,2,1,0:T(8,128)}, f32[16,4,8,128]{3,2,1,0:T(8,128)}) custom-call(s32[2]{0:T(128)} %add_convert_fusion.1.edge_ref, bf16[1024,512]{1,0:T(8,128)(2,1)} %q_ref.3, bf16[1152,512]{1,0:T(8,128)(2,1)} %get-tuple-element.14.k_ref, bf16[1152,512]{1,0:T(8,128)(2,1)} %get-tuple-element.13.v_ref, ...), custom_call_target="tpu_custom_call" | custom-call | flops 20000000000 | bytes 8000000 | tf_op jit(solution)/shard_map/attend_near/pallas_call | solution.py:162
  239.2 17.3 %attend_far.1 = bf16[1024,512]{1,0:T(8,128)(2,1)} custom-call(s32[384]{0:T(512)} %fusion.70.slot_ref, bf16[1024,512]{1,0:T(8,128)(2,1)} %q_ref.3, bf16[384,64,128]{2,1,0:T(8,128)(2,1)} %bitcast.1.rand_ref, f32[16,4,64,128]{3,2,1,0:T(8,128)} %get-tuple-element.7.acc_ref, f32[16,4,8,128]{3,2,1,0:T(8,128)} %get-tuple-element.8.stat_ref), custom_call_target="tpu_custom_call" | custom-call | flops 15000000512 | bytes 10000000 | tf_op jit(solution)/shard_map/attend_far/pallas_call | solution.py:191
  256.5 1.5 select_dynamic-update-slice_fusion.1
  258.0 1.5 select_dynamic-update-slice_fusion
  259.5 1.1 constant_dynamic-slice_fusion.1
  260.5 3.7 %collective-permute-start.2 = (bf16[512,512]{1,0:T(8,128)(2,1)S(1)}, bf16[512,512]{1,0:T(8,128)(2,1)S(1)}, u32[]{:S(2)}, u32[]{:S(2)}) collective-permute-start(bf16[512,512]{1,0:T(8,128)(2,1)S(1)} %constant_dynamic-slice_fusion.1), channel_id=1, source_target_pairs={{0,1},{1,0},{2,3},{3,2},{4,5},{5,4},{6,7},{7,6},{8,9},{9,8},{10,11... | collective-permute-start | bytes 1572872 | tf_op jit(solution)/shard_map/ppermute | solution.py:378
  264.3 1.9 fusion.48
  266.2 2.1 convert_reduce_fusion
  268.4 0.4 fusion.20
  268.8 9.5 %fusion.29 = f32[512,1024]{1,0:T(8,128)} fusion(bf16[2048,1024]{1,0:T(8,128)(2,1)} %param.19, bf16[1024,2048]{1,0:T(8,128)(2,1)} %param.18, bf16[512,1024]{1,0:T(8,128)(2,1)S(1)} %get-tuple-element.33, f32[1024]{0:T(1024)S(1)} %copy-done.7, f32[512]{0:T(512)S(1)} %add_rsqrt_fusion, f32[512]{0:T(512)S(1)} %broadcast_multiply_fusion), kind=kOutput, calls=%fused_computation.36 | convolution fusion | flops 4307025920 | bytes 11542528 | tf_op jit(solution)/shard_map/dot_general | solution.py:396
  278.3 8.7 %fusion.24 = bf16[512,1024]{1,0:T(8,128)(2,1)S(1)} fusion(f32[512,1024]{1,0:T(8,128)} %fusion.29, bf16[512,1024]{1,0:T(8,128)(2,1)S(1)} %get-tuple-element.33, bf16[2048,1024]{1,0:T(8,128)(2,1)} %collective-permute-done.5, bf16[1024,2048]{1,0:T(8,128)(2,1)} %collective-permute-done.4, f32[1024]{0:T(1024)S(1)} %copy-done.7, f32[512]{0:T(512)S(1)} %add_rsqrt_fusion, ...), kind=kOutput, calls=%fused_computation.33 | convolution fusion | flops 4309123072 | bytes 12591104 | tf_op jit(solution)/shard_map/dot_general | solution.py:396
  287.2 1.9 collective-permute-done.6
  289.3 1.0 pad_maximum_fusion.2
  (63 shorter events, 3.5 us)
Async XLA Ops:
  6.5 25.4 %copy-start.2 = (bf16[1024,512]{1,0:T(8,128)(2,1)S(1)}, bf16[1024,512]{1,0:T(8,128)(2,1)}, u32[]{:S(2)}) copy-start(bf16[1024,512]{1,0:T(8,128)(2,1)} %value_ref.1) | copy-start | bytes 3145732
  8.8 23.6 %copy-start = (bf16[1024,512]{1,0:T(8,128)(2,1)S(1)}, bf16[1024,512]{1,0:T(8,128)(2,1)}, u32[]{:S(2)}) copy-start(bf16[1024,512]{1,0:T(8,128)(2,1)} %key_ref.1) | copy-start | bytes 3145732
  26.6 15.3 %all-to-all-start.2 = ((bf16[16,24,512]{2,1,0:T(8,128)(2,1)}), bf16[16,24,512]{2,1,0:T(8,128)(2,1)S(1)}, u32[]{:S(2)}, u32[]{:S(2)}) async-start(bf16[16,24,512]{2,1,0:T(8,128)(2,1)} %broadcast_in_dim.22), calls=%async_computation.2 | async-start | bytes 786432 | tf_op jit(solution)/shard_map/all_to_all | solution.py:287
  44.6 7.8 %copy-start.6 = (s32[16,384]{1,0:T(8,128)S(1)}, s32[16,384]{1,0:T(8,128)}, u32[]{:S(2)}) copy-start(s32[16,384]{1,0:T(8,128)} %reshape.258) | copy-start | bytes 73732
  47.3 12.3 %all-to-all-start.3 = ((bf16[16,1,64,128]{3,2,1,0:T(8,128)(2,1)}), bf16[16,1,64,128]{3,2,1,0:T(8,128)(2,1)S(1)}, u32[]{:S(2)}, u32[]{:S(2)}) async-start(bf16[16,1,64,128]{3,2,1,0:T(8,128)(2,1)} %copy.40), calls=%async_computation.3 | async-start | bytes 524288 | tf_op jit(solution)/shard_map/all_to_all | solution.py:325
  61.2 12.7 %all-to-all-start.4 = ((bf16[16,2,2048]{2,1,0:T(2,128)(2,1)}), bf16[16,2,2048]{2,1,0:T(2,128)(2,1)S(1)}, u32[]{:S(2)}, u32[]{:S(2)}) async-start(bf16[16,2,2048]{2,1,0:T(2,128)(2,1)} %reshape.270), calls=%async_computation.4 | async-start | bytes 262144 | tf_op jit(solution)/shard_map/all_to_all | solution.py:350
  73.9 6.7 %copy-start.1 = (bf16[1024,512]{1,0:T(8,128)(2,1)S(1)}, bf16[1024,512]{1,0:T(8,128)(2,1)}, u32[]{:S(2)}) copy-start(bf16[1024,512]{1,0:T(8,128)(2,1)} %key_ref.1) | copy-start | bytes 3145732
  73.9 6.7 %copy-start.3 = (bf16[1024,512]{1,0:T(8,128)(2,1)S(1)}, bf16[1024,512]{1,0:T(8,128)(2,1)}, u32[]{:S(2)}) copy-start(bf16[1024,512]{1,0:T(8,128)(2,1)} %value_ref.1) | copy-start | bytes 3145732
  73.9 13.3 %copy-start.4 = (bf16[512,1024]{1,0:T(8,128)(2,1)S(1)}, bf16[512,1024]{1,0:T(8,128)(2,1)}, u32[]{:S(2)}) copy-start(bf16[512,1024]{1,0:T(8,128)(2,1)} %param.16) | copy-start | bytes 3145732
  74.0 165.3 %all-to-all-start = ((bf16[16,24,64,128]{3,2,1,0:T(8,128)(2,1)}), bf16[16,24,64,128]{3,2,1,0:T(8,128)(2,1)}, u32[]{:S(2)}, u32[]{:S(2)}) async-start(bf16[16,24,64,128]{3,2,1,0:T(8,128)(2,1)} %bitcast.71), calls=%async_computation | async-start | bytes 12582912 | tf_op jit(solution)/shard_map/all_to_all | solution.py:325
  81.3 136.8 %collective-permute-start.1 = (bf16[2,64,512]{2,1,0:T(8,128)(2,1)}, bf16[2,64,512]{2,1,0:T(8,128)(2,1)S(1)}, u32[]{:S(2)}, u32[]{:S(2)}) collective-permute-start(bf16[2,64,512]{2,1,0:T(8,128)(2,1)} %get-tuple-element.16), channel_id=1, source_target_pairs={{2,0},{4,2},{6,4},{8,6},{10,8},{12,10},{14,12},{16,14},{18,16},{20... | collective-permute-start | bytes 393224 | tf_op jit(solution)/shard_map/ppermute | solution.py:274
  85.3 135.3 %collective-permute-start = (bf16[2,64,512]{2,1,0:T(8,128)(2,1)S(1)}, bf16[2,64,512]{2,1,0:T(8,128)(2,1)}, u32[]{:S(2)}, u32[]{:S(2)}) collective-permute-start(bf16[2,64,512]{2,1,0:T(8,128)(2,1)S(1)} %get-tuple-element.15), channel_id=1, source_target_pairs={{0,2},{2,4},{4,6},{6,8},{8,10},{10,12},{12,14},{14,16},{16,18},{18... | collective-permute-start | bytes 393224 | tf_op jit(solution)/shard_map/ppermute | solution.py:273
  87.2 179.0 %collective-permute-start.3 = (bf16[512,1024]{1,0:T(8,128)(2,1)S(1)}, bf16[512,1024]{1,0:T(8,128)(2,1)}, u32[]{:S(2)}, u32[]{:S(2)}) collective-permute-start(bf16[512,1024]{1,0:T(8,128)(2,1)S(1)} %copy-done.4), channel_id=1, source_target_pairs={{0,1},{1,0},{2,3},{3,2},{4,5},{5,4},{6,7},{7,6},{8,9},{9,8},{10,11... | collective-permute-start | bytes 3145736 | tf_op jit(solution)/shard_map/ppermute | solution.py:330
  90.3 188.0 %collective-permute-start.5 = (bf16[2048,1024]{1,0:T(8,128)(2,1)}, bf16[2048,1024]{1,0:T(8,128)(2,1)}, u32[]{:S(2)}, u32[]{:S(2)}) collective-permute-start(bf16[2048,1024]{1,0:T(8,128)(2,1)} %param.19), channel_id=1, source_target_pairs={{0,1},{1,0},{2,3},{3,2},{4,5},{5,4},{6,7},{7,6},{8,9},{9,8},{10,11... | collective-permute-start | bytes 12582920 | tf_op jit(solution)/shard_map/ppermute | solution.py:332
  90.3 187.9 %collective-permute-start.4 = (bf16[1024,2048]{1,0:T(8,128)(2,1)}, bf16[1024,2048]{1,0:T(8,128)(2,1)}, u32[]{:S(2)}, u32[]{:S(2)}) collective-permute-start(bf16[1024,2048]{1,0:T(8,128)(2,1)} %param.18), channel_id=1, source_target_pairs={{0,1},{1,0},{2,3},{3,2},{4,5},{5,4},{6,7},{7,6},{8,9},{9,8},{10,11... | collective-permute-start | bytes 12582920 | tf_op jit(solution)/shard_map/ppermute | solution.py:331
  260.5 5.7 %collective-permute-start.2 = (bf16[512,512]{1,0:T(8,128)(2,1)S(1)}, bf16[512,512]{1,0:T(8,128)(2,1)S(1)}, u32[]{:S(2)}, u32[]{:S(2)}) collective-permute-start(bf16[512,512]{1,0:T(8,128)(2,1)S(1)} %constant_dynamic-slice_fusion.1), channel_id=1, source_target_pairs={{0,1},{1,0},{2,3},{3,2},{4,5},{5,4},{6,7},{7,6},{8,9},{9,8},{10,11... | collective-permute-start | bytes 1572872 | tf_op jit(solution)/shard_map/ppermute | solution.py:378
  264.3 1.9 copy-start.5
  266.2 2.6 copy-start.7
  287.1 2.0 collective-permute-start.6

commit v4 on v3

--- a/solution.py
+++ b/solution.py
@@ -262,7 +262,7 @@
     )
     chosen = jnp.sum(jnp.where(pick_table, source[:, None, :], 0), axis=2)
     my_rank = jnp.sum(jnp.where(by_owner, ranks[GROUP:], 0), axis=0)
-    slots = owner * capacity + my_rank
+    slots = owner * (capacity + 1) + my_rank
 
     groups = [
         list(range(start, start + GROUP)) for start in range(0, shard_count, GROUP)
@@ -319,13 +319,16 @@
     ).astype(jnp.bfloat16)
     part = part.reshape(GROUP, 1, merge_rows, 2 * HD)
 
-    tiles = pack(chosen.reshape(slot_count), key_rows, value_rows)
-    tiles = tiles.reshape(GROUP, capacity, BLK, 2 * HD)
-    received, parts = (
-        lax.all_to_all(block, "seq", 0, 0, axis_index_groups=groups, tiled=True)
-        for block in (tiles, part)
-    )
-    received = received.reshape(slot_count, BLK, 2 * HD)
+    chosen = jnp.pad(chosen, ((0, 0), (0, 1)))
+    tiles = pack(chosen.reshape(GROUP * (capacity + 1)), key_rows, value_rows)
+    tiles = tiles.reshape(GROUP, capacity + 1, BLK, 2 * HD)
+    tiles = lax.dynamic_update_slice_in_dim(tiles, part, capacity, 1)
+    tiles, below, above = lax.optimization_barrier((tiles, below, above))
+    received = lax.all_to_all(
+        tiles, "seq", 0, 0, axis_index_groups=groups, tiled=True
+    )
+    parts = received[:, capacity]
+    received = received.reshape(GROUP * (capacity + 1), BLK, 2 * HD)
 
     other_out = lax.ppermute(out_weight, "mp", swap)
     other_up = lax.ppermute(up_weight, "mp", swap)
@@ -337,7 +340,7 @@
         edges, query_rows, padded[0], padded[1], global_k, global_v
     )
 
-    parts = parts[:, 0].astype(jnp.float32)
+    parts = parts.astype(jnp.float32)
     merged = merge_parts(
         parts[..., HD], parts[..., HD + 1] + parts[..., HD + 2], parts[..., :HD]
     )

time: 292 us -> 263 us (0.901)
  waiting for transfers between devices: 143 us -> 120 us
  blocking collectives: 16.8 us -> 0 us
  starting transfers between devices: 35.7 us -> 40 us
  other arithmetic: 12.4 us -> 16.5 us
    ppermute x1, waiting for transfers between devices: 126 us -> 0.01 us  [local(): above = lax.ppermute(both[:, :BLK], 'seq', backward)]
    all_to_all x2, waiting for transfers between devices: 6.88 us -> 118 us  [the longest x1 118 us: local(): lax.all_to_all(tiles, 'seq', 0, 0, axis_index_groups=groups, tiled=True)]
    all_to_all x1 -> x0, blocking collectives: 16.8 us -> none  [local(): shares = lax.all_to_all(shares, 'seq', 0, 0, tiled=True)]
    all_to_all x1, waiting for transfers between devices: 5.96 us -> 0.01 us  [local(): lax.all_to_all(jnp.broadcast_to(share[None], (shard_count,) + share.shape...]
    all_to_all x1, starting transfers between devices: 5.36 us -> 8.79 us  [local(): lax.all_to_all(jnp.broadcast_to(merged_rows[None], (GROUP,) + merged_rows...]
  transfers between devices with their start and end apart: 11 -> 11, of which waited for: 5 -> 2; matrix products, arithmetic and copies ran while one was open for 10% -> 16% of each run, Pallas kernels for 13% -> 15%
where the time goes in v4:
time: 263 us; the launch traced here: 260 us
  waiting for transfers between devices  120 us (46%)
  starting transfers between devices  40 us (15%)
  Pallas kernels  38.3 us (15%)
  matrix products  24.9 us (9%)
  other arithmetic  16.5 us (6%)
  local copies, waits for them, and re-layouts  15 us (6%)
  between operations  5.56 us (2%)
    all_to_all x1, waiting for transfers between devices, local(): lax.all_to_all(tiles, 'seq', 0, 0, axis_index_groups=groups, tiled=True)  118 us
    dot_general x2, matrix products, local(): total = total + jnp.dot(hidden, down, preferred_element_type=jnp.float32)  18.2 us
    pallas_call x1, Pallas kernels, attend_far(): pl.pallas_call(far_kernel, out_shape=jax.ShapeDtypeStruct((tokens, width)...  17.3 us
    pallas_call x1, Pallas kernels, attend_near(): pl.pallas_call(near_kernel, out_shape=(jax.ShapeDtypeStruct((QB_DEV, pair...  14.5 us
    all_to_all x1, starting transfers between devices, local(): lax.all_to_all(jnp.broadcast_to(merged_rows[None], (GROUP,) + merged_rows...  8.79 us
    all_to_all x1, starting transfers between devices, local(): lax.all_to_all(tiles, 'seq', 0, 0, axis_index_groups=groups, tiled=True)  6.63 us
    all_to_all x1, starting transfers between devices, local(): shares = lax.all_to_all(shares, 'seq', 0, 0, tiled=True)  6.55 us
    pallas_call x1, Pallas kernels, pack(): pl.pallas_call(pack_kernel, out_shape=jax.ShapeDtypeStruct((slots, BLK, 2...  6.41 us
  transfers between devices with their start and end apart: 11, of which 2 were waited for; matrix products, arithmetic and copies ran while one was open for 16% of the time, Pallas kernels for 15%

profile of v4, /device:TPU:17, one launch (start us, length us, event | category | flops | bytes accessed | tf_op | source)
XLA Modules:
  0.0 260.5 jit_solution(49983191081319028)
XLA Ops:
  0.0 1.3 fusion.101
  6.6 2.3 pad_maximum_fusion
  9.0 0.8 pad_maximum_fusion.3
  9.8 6.6 %all-to-all-start = ((bf16[16,24,512]{2,1,0:T(8,128)(2,1)}), bf16[16,24,512]{2,1,0:T(8,128)(2,1)S(1)}, u32[]{:S(2)}, u32[]{:S(2)}) async-start(bf16[16,24,512]{2,1,0:T(8,128)(2,1)} %bitcast.6), calls=%async_computation | async-start | bytes 786432 | tf_op jit(solution)/shard_map/all_to_all | solution.py:285
  16.3 0.7 pad_maximum_fusion.4
  17.1 3.1 %collective-permute-start = (bf16[2,64,512]{2,1,0:T(8,128)(2,1)}, bf16[2,64,512]{2,1,0:T(8,128)(2,1)}, u32[]{:S(2)}, u32[]{:S(2)}) collective-permute-start(bf16[2,64,512]{2,1,0:T(8,128)(2,1)} %get-tuple-element.22), channel_id=1, source_target_pairs={{0,2},{2,4},{4,6},{6,8},{8,10},{10,12},{12,14},{14,16},{16,18},{18... | collective-permute-start | bytes 393224 | tf_op jit(solution)/shard_map/ppermute | solution.py:273
  20.1 4.0 %collective-permute-start.1 = (bf16[2,64,512]{2,1,0:T(8,128)(2,1)}, bf16[2,64,512]{2,1,0:T(8,128)(2,1)}, u32[]{:S(2)}, u32[]{:S(2)}) collective-permute-start(bf16[2,64,512]{2,1,0:T(8,128)(2,1)} %get-tuple-element.21), channel_id=1, source_target_pairs={{2,0},{4,2},{6,4},{8,6},{10,8},{12,10},{14,12},{16,14},{18,16},{20... | collective-permute-start | bytes 393224 | tf_op jit(solution)/shard_map/ppermute | solution.py:274
  24.2 1.2 copy.36
  25.3 1.1 reshape.258
  26.4 1.2 fusion.76
  27.7 1.3 fusion.53
  29.1 0.8 broadcast_in_dim.22
  29.8 5.2 %all-to-all-start.1 = ((bf16[16,24,512]{2,1,0:T(8,128)(2,1)}), bf16[16,24,512]{2,1,0:T(8,128)(2,1)S(1)}, u32[]{:S(2)}, u32[]{:S(2)}) async-start(bf16[16,24,512]{2,1,0:T(8,128)(2,1)} %broadcast_in_dim.22), calls=%async_computation.1 | async-start | bytes 786432 | tf_op jit(solution)/shard_map/all_to_all | solution.py:287
  35.0 0.6 add_select_fusion.2
  35.6 0.5 copy.39
  36.2 0.5 copy.38
  36.7 0.9 convolution_convert_fusion
  37.6 0.8 fusion.55
  38.7 0.7 reshape.259.index_ref
  39.4 6.4 %pack.1 = bf16[400,64,128]{2,1,0:T(8,128)(2,1)} custom-call(s32[400]{0:T(512)} %reshape.259.index_ref, bf16[1024,512]{1,0:T(8,128)(2,1)} %key_ref.1, bf16[1024,512]{1,0:T(8,128)(2,1)} %value_ref.1), custom_call_target="tpu_custom_call" | custom-call | tf_op jit(solution)/shard_map/pack/pallas_call | solution.py:54
  45.8 0.7 slice_bitcast_fusion.2
  46.7 0.8 multiply_reduce_fusion
  47.5 0.9 fusion.16
  48.4 1.0 fusion.43
  49.9 0.5 copy.41
  50.4 0.8 constant_dynamic-update-slice_fusion.4
  51.2 6.6 %all-to-all-start.2 = ((bf16[16,25,64,128]{3,2,1,0:T(8,128)(2,1)}), bf16[16,25,64,128]{3,2,1,0:T(8,128)(2,1)}, u32[]{:S(2)}, u32[]{:S(2)}) async-start(bf16[16,25,64,128]{3,2,1,0:T(8,128)(2,1)} %constant_dynamic-update-slice_fusion.4), calls=%async_computation.2 | async-start | bytes 13107200 | tf_op jit(solution)/shard_map/all_to_all | solution.py:327
  57.8 3.0 %collective-permute-start.3 = (bf16[512,1024]{1,0:T(8,128)(2,1)S(1)}, bf16[512,1024]{1,0:T(8,128)(2,1)}, u32[]{:S(2)}, u32[]{:S(2)}) collective-permute-start(bf16[512,1024]{1,0:T(8,128)(2,1)S(1)} %copy-done.4), channel_id=1, source_target_pairs={{0,1},{1,0},{2,3},{3,2},{4,5},{5,4},{6,7},{7,6},{8,9},{9,8},{10,11... | collective-permute-start | bytes 3145736 | tf_op jit(solution)/shard_map/ppermute | solution.py:333
  61.3 0.6 add_convert_fusion.1.edge_ref
  61.9 0.5 fusion.70.slot_ref
  62.5 1.1 pad_maximum_fusion.1
  63.6 1.6 slice_bitcast_fusion
  65.2 14.5 %attend_near.1 = (f32[16,4,64,128]{3,2,1,0:T(8,128)}, f32[16,4,8,128]{3,2,1,0:T(8,128)}) custom-call(s32[2]{0:T(128)} %add_convert_fusion.1.edge_ref, bf16[1024,512]{1,0:T(8,128)(2,1)} %q_ref.3, bf16[1152,512]{1,0:T(8,128)(2,1)} %get-tuple-element.20.k_ref, bf16[1152,512]{1,0:T(8,128)(2,1)} %get-tuple-element.19.v_ref, ...), custom_call_target="tpu_custom_call" | custom-call | flops 20000000000 | bytes 8000000 | tf_op jit(solution)/shard_map/attend_near/pallas_call | solution.py:162
  79.7 118.4 %all-to-all-done.2 = bf16[16,25,64,128]{3,2,1,0:T(8,128)(2,1)} async-done(((bf16[16,25,64,128]{3,2,1,0:T(8,128)(2,1)}), bf16[16,25,64,128]{3,2,1,0:T(8,128)(2,1)}, u32[]{:S(2)}, u32[]{:S(2)}) %all-to-all-start.2) | async-done | bytes 6553632 | tf_op jit(solution)/shard_map/all_to_all | solution.py:327
  198.1 1.0 slice.89
  199.8 0.9 reshape.270
  200.7 8.8 %all-to-all-start.3 = ((bf16[16,2,2048]{2,1,0:T(2,128)(2,1)}), bf16[16,2,2048]{2,1,0:T(2,128)(2,1)S(1)}, u32[]{:S(2)}, u32[]{:S(2)}) async-start(bf16[16,2,2048]{2,1,0:T(2,128)(2,1)} %reshape.270), calls=%async_computation.3 | async-start | bytes 262144 | tf_op jit(solution)/shard_map/all_to_all | solution.py:353
  209.5 17.3 %attend_far.1 = bf16[1024,512]{1,0:T(8,128)(2,1)} custom-call(s32[384]{0:T(512)} %fusion.70.slot_ref, bf16[1024,512]{1,0:T(8,128)(2,1)} %q_ref.3, bf16[400,64,128]{2,1,0:T(8,128)(2,1)} %bitcast.13.rand_ref, f32[16,4,64,128]{3,2,1,0:T(8,128)} %get-tuple-element.13.acc_ref, f32[16,4,8,128]{3,2,1,0:T(8,128)} %get-tuple-element.14.stat_ref), custom_call_target="tpu_custom_call" | custom-call | flops 15000000512 | bytes 10000000 | tf_op jit(solution)/shard_map/attend_far/pallas_call | solution.py:191
  228.2 1.5 select_dynamic-update-slice_fusion.1
  229.7 1.5 select_dynamic-update-slice_fusion
  231.1 1.1 constant_dynamic-slice_fusion.1
  232.2 2.2 collective-permute-start.2
  234.4 1.9 fusion.48
  236.3 2.1 convert_reduce_fusion
  238.9 9.5 %fusion.29 = f32[512,1024]{1,0:T(8,128)} fusion(bf16[2048,1024]{1,0:T(8,128)(2,1)} %param.19, bf16[1024,2048]{1,0:T(8,128)(2,1)} %param.18, bf16[512,1024]{1,0:T(8,128)(2,1)S(1)} %get-tuple-element.39, f32[1024]{0:T(1024)S(1)} %copy-done.7, f32[512]{0:T(512)S(1)} %add_rsqrt_fusion, f32[512]{0:T(512)S(1)} %broadcast_multiply_fusion), kind=kOutput, calls=%fused_computation.36 | convolution fusion | flops 4307025920 | bytes 11542528 | tf_op jit(solution)/shard_map/dot_general | solution.py:399
  248.4 8.7 %fusion.24 = bf16[512,1024]{1,0:T(8,128)(2,1)S(1)} fusion(f32[512,1024]{1,0:T(8,128)} %fusion.29, bf16[512,1024]{1,0:T(8,128)(2,1)S(1)} %get-tuple-element.39, bf16[2048,1024]{1,0:T(8,128)(2,1)} %collective-permute-done.5, bf16[1024,2048]{1,0:T(8,128)(2,1)} %collective-permute-done.4, f32[1024]{0:T(1024)S(1)} %copy-done.7, f32[512]{0:T(512)S(1)} %add_rsqrt_fusion, ...), kind=kOutput, calls=%fused_computation.33 | convolution fusion | flops 4309123072 | bytes 12591104 | tf_op jit(solution)/shard_map/dot_general | solution.py:399
  257.3 1.9 collective-permute-done.6
  259.4 1.0 pad_maximum_fusion.2
  (65 shorter events, 4.5 us)
Async XLA Ops:
  6.5 9.8 %copy-start = (bf16[1024,512]{1,0:T(8,128)(2,1)S(1)}, bf16[1024,512]{1,0:T(8,128)(2,1)}, u32[]{:S(2)}) copy-start(bf16[1024,512]{1,0:T(8,128)(2,1)} %key_ref.1) | copy-start | bytes 3145732
  6.5 9.8 %copy-start.2 = (bf16[1024,512]{1,0:T(8,128)(2,1)S(1)}, bf16[1024,512]{1,0:T(8,128)(2,1)}, u32[]{:S(2)}) copy-start(bf16[1024,512]{1,0:T(8,128)(2,1)} %value_ref.1) | copy-start | bytes 3145732
  9.8 19.2 %all-to-all-start = ((bf16[16,24,512]{2,1,0:T(8,128)(2,1)}), bf16[16,24,512]{2,1,0:T(8,128)(2,1)S(1)}, u32[]{:S(2)}, u32[]{:S(2)}) async-start(bf16[16,24,512]{2,1,0:T(8,128)(2,1)} %bitcast.6), calls=%async_computation | async-start | bytes 786432 | tf_op jit(solution)/shard_map/all_to_all | solution.py:285
  17.1 34.1 %collective-permute-start = (bf16[2,64,512]{2,1,0:T(8,128)(2,1)}, bf16[2,64,512]{2,1,0:T(8,128)(2,1)}, u32[]{:S(2)}, u32[]{:S(2)}) collective-permute-start(bf16[2,64,512]{2,1,0:T(8,128)(2,1)} %get-tuple-element.22), channel_id=1, source_target_pairs={{0,2},{2,4},{4,6},{6,8},{8,10},{10,12},{12,14},{14,16},{16,18},{18... | collective-permute-start | bytes 393224 | tf_op jit(solution)/shard_map/ppermute | solution.py:273
  20.1 31.1 %collective-permute-start.1 = (bf16[2,64,512]{2,1,0:T(8,128)(2,1)}, bf16[2,64,512]{2,1,0:T(8,128)(2,1)}, u32[]{:S(2)}, u32[]{:S(2)}) collective-permute-start(bf16[2,64,512]{2,1,0:T(8,128)(2,1)} %get-tuple-element.21), channel_id=1, source_target_pairs={{2,0},{4,2},{6,4},{8,6},{10,8},{12,10},{14,12},{16,14},{18,16},{20... | collective-permute-start | bytes 393224 | tf_op jit(solution)/shard_map/ppermute | solution.py:274
  29.8 16.0 %all-to-all-start.1 = ((bf16[16,24,512]{2,1,0:T(8,128)(2,1)}), bf16[16,24,512]{2,1,0:T(8,128)(2,1)S(1)}, u32[]{:S(2)}, u32[]{:S(2)}) async-start(bf16[16,24,512]{2,1,0:T(8,128)(2,1)} %broadcast_in_dim.22), calls=%async_computation.1 | async-start | bytes 786432 | tf_op jit(solution)/shard_map/all_to_all | solution.py:287
  51.2 6.7 %copy-start.4 = (bf16[512,1024]{1,0:T(8,128)(2,1)S(1)}, bf16[512,1024]{1,0:T(8,128)(2,1)}, u32[]{:S(2)}) copy-start(bf16[512,1024]{1,0:T(8,128)(2,1)} %param.16) | copy-start | bytes 3145732
  51.2 10.7 %copy-start.6 = (s32[384]{0:T(512)S(1)}, s32[384]{0:T(512)}, u32[]{:S(2)}) copy-start(s32[384]{0:T(512)} %get-tuple-element.15) | copy-start | bytes 4612
  51.2 11.3 %copy-start.1 = (bf16[1024,512]{1,0:T(8,128)(2,1)S(1)}, bf16[1024,512]{1,0:T(8,128)(2,1)}, u32[]{:S(2)}) copy-start(bf16[1024,512]{1,0:T(8,128)(2,1)} %key_ref.1) | copy-start | bytes 3145732
  51.2 11.3 %copy-start.3 = (bf16[1024,512]{1,0:T(8,128)(2,1)S(1)}, bf16[1024,512]{1,0:T(8,128)(2,1)}, u32[]{:S(2)}) copy-start(bf16[1024,512]{1,0:T(8,128)(2,1)} %value_ref.1) | copy-start | bytes 3145732
  51.2 146.9 %all-to-all-start.2 = ((bf16[16,25,64,128]{3,2,1,0:T(8,128)(2,1)}), bf16[16,25,64,128]{3,2,1,0:T(8,128)(2,1)}, u32[]{:S(2)}, u32[]{:S(2)}) async-start(bf16[16,25,64,128]{3,2,1,0:T(8,128)(2,1)} %constant_dynamic-update-slice_fusion.4), calls=%async_computation.2 | async-start | bytes 13107200 | tf_op jit(solution)/shard_map/all_to_all | solution.py:327
  57.8 178.5 %collective-permute-start.3 = (bf16[512,1024]{1,0:T(8,128)(2,1)S(1)}, bf16[512,1024]{1,0:T(8,128)(2,1)}, u32[]{:S(2)}, u32[]{:S(2)}) collective-permute-start(bf16[512,1024]{1,0:T(8,128)(2,1)S(1)} %copy-done.4), channel_id=1, source_target_pairs={{0,1},{1,0},{2,3},{3,2},{4,5},{5,4},{6,7},{7,6},{8,9},{9,8},{10,11... | collective-permute-start | bytes 3145736 | tf_op jit(solution)/shard_map/ppermute | solution.py:333
  60.8 187.6 %collective-permute-start.5 = (bf16[2048,1024]{1,0:T(8,128)(2,1)}, bf16[2048,1024]{1,0:T(8,128)(2,1)}, u32[]{:S(2)}, u32[]{:S(2)}) collective-permute-start(bf16[2048,1024]{1,0:T(8,128)(2,1)} %param.19), channel_id=1, source_target_pairs={{0,1},{1,0},{2,3},{3,2},{4,5},{5,4},{6,7},{7,6},{8,9},{9,8},{10,11... | collective-permute-start | bytes 12582920 | tf_op jit(solution)/shard_map/ppermute | solution.py:335
  60.9 187.5 %collective-permute-start.4 = (bf16[1024,2048]{1,0:T(8,128)(2,1)}, bf16[1024,2048]{1,0:T(8,128)(2,1)}, u32[]{:S(2)}, u32[]{:S(2)}) collective-permute-start(bf16[1024,2048]{1,0:T(8,128)(2,1)} %param.18), channel_id=1, source_target_pairs={{0,1},{1,0},{2,3},{3,2},{4,5},{5,4},{6,7},{7,6},{8,9},{9,8},{10,11... | collective-permute-start | bytes 12582920 | tf_op jit(solution)/shard_map/ppermute | solution.py:334
  200.7 26.1 %all-to-all-start.3 = ((bf16[16,2,2048]{2,1,0:T(2,128)(2,1)}), bf16[16,2,2048]{2,1,0:T(2,128)(2,1)S(1)}, u32[]{:S(2)}, u32[]{:S(2)}) async-start(bf16[16,2,2048]{2,1,0:T(2,128)(2,1)} %reshape.270), calls=%async_computation.3 | async-start | bytes 262144 | tf_op jit(solution)/shard_map/all_to_all | solution.py:353
  232.2 4.1 %collective-permute-start.2 = (bf16[512,512]{1,0:T(8,128)(2,1)S(1)}, bf16[512,512]{1,0:T(8,128)(2,1)S(1)}, u32[]{:S(2)}, u32[]{:S(2)}) collective-permute-start(bf16[512,512]{1,0:T(8,128)(2,1)S(1)} %constant_dynamic-slice_fusion.1), channel_id=1, source_target_pairs={{0,1},{1,0},{2,3},{3,2},{4,5},{5,4},{6,7},{7,6},{8,9},{9,8},{10,11... | collective-permute-start | bytes 1572872 | tf_op jit(solution)/shard_map/ppermute | solution.py:381
  234.4 1.9 copy-start.5
  236.3 2.6 %copy-start.7 = (f32[1024]{0:T(1024)S(1)}, f32[1024]{0:T(1024)}, u32[]{:S(2)}) copy-start(f32[1024]{0:T(1024)} %param.17) | copy-start | bytes 12292
  257.2 2.0 collective-permute-start.6
